TPU v7x, 128 devices: a whole 4x4x4 slice. The times are simulated.
128 devices in a mesh: gr: 16 (over z, y_lo, core), gc: 8 (over y_hi, x).
Axes of the slice: x: 4, y: 4 (y_hi: 2, y_lo: 2; y = y_hi * 2 + y_lo), z: 4, core: 2. Of those that a mesh axis runs over, the one named last changes fastest.
Arguments:
- features: bfloat16 [65536, 128], P(('gr', 'gc')), may hold values from -6 to 6
- weight: bfloat16 [128, 128], replicated, may hold values from -0.5 to 0.5
- cotangent: bfloat16 [65536, 128], P(('gr', 'gc')), may hold values from -6 to 6
- tiles: bfloat16 [16, 8, 736, 128, 128], P('gr', 'gc')
- tile_rows: int32 [16, 8, 736], P('gr', 'gc'), may hold values from 0 to 31
- tile_cols: int32 [16, 8, 736], P('gr', 'gc'), may hold values from 0 to 63
- tile_counts: int32 [16, 8], P('gr', 'gc'), may hold values from 184 to 736, as said below
Outputs:
- output: bfloat16 [65536, 128], P(('gr', 'gc'))
- grad_features: bfloat16 [65536, 128], P(('gr', 'gc'))
- grad_weight: float32 [128, 128], replicated
Inputs may be any that keep to these rules, and one draw needn't show every extreme that they name: `tile_counts`: some grid block holds exactly 736 live slots. `tile_rows`: positions may repeat within a block. `tile_cols`: positions may repeat within a block.
All inputs are finite; a program needn't handle non-finite values.
Results may differ from a plain program's by a relative error of at most 0.0075.
Values may be sent and summed in bfloat16 or wider, within the bound.
No kernel may reach another device: no remote copies, remote signals or barrier semaphores. Data moves between devices by JAX's collectives and lax.ppermute only.
A program may use at most 128 MiB of HBM per device.

v0:
```python
import math

import jax
import jax.numpy as jnp
from jax import lax
from jax.sharding import PartitionSpec as P


def gelu_pair(pre_act):
    coeff = 0.7978845608028654
    cubed = pre_act * pre_act * pre_act
    tanh_val = jnp.tanh(coeff * (pre_act + 0.044715 * cubed))
    gelu_value = 0.5 * pre_act * (1.0 + tanh_val)
    gelu_slope = 0.5 * (1.0 + tanh_val) + 0.5 * pre_act * (1.0 - tanh_val * tanh_val) * coeff * (
        1.0 + 3.0 * 0.044715 * pre_act * pre_act
    )
    return (gelu_value, gelu_slope)


def tile_pass(
    blocks, source_ids, target_ids, tile_count, table, out_tiles, transposed, loop_turns, slot_group
):
    tile_size = blocks.shape[1]
    feat_width = table.shape[2]
    table_tiles = table.shape[0]
    table_flat = table.reshape(table_tiles, tile_size * feat_width)
    table_index = jnp.arange(table_tiles, dtype=jnp.int32)
    target_index = jnp.arange(out_tiles, dtype=jnp.int32)

    def advance(group_index, totals):
        first_slot = group_index * slot_group
        tile_block = lax.dynamic_slice_in_dim(blocks, first_slot, slot_group, 0)
        source_part = lax.dynamic_slice_in_dim(source_ids, first_slot, slot_group, 0)
        target_part = lax.dynamic_slice_in_dim(target_ids, first_slot, slot_group, 0)
        pick_matrix = (source_part[:, None] == table_index[None, :]).astype(jnp.bfloat16)
        picked = jnp.dot(pick_matrix, table_flat, preferred_element_type=jnp.float32).astype(
            jnp.bfloat16
        )
        picked = picked.reshape(slot_group, tile_size, feat_width)
        if transposed:
            products = jnp.einsum(
                "sab,saf->sbf", tile_block, picked, preferred_element_type=jnp.float32
            )
        else:
            products = jnp.einsum(
                "sab,sbf->saf", tile_block, picked, preferred_element_type=jnp.float32
            )
        slot_index = first_slot + jnp.arange(slot_group, dtype=jnp.int32)
        live_mask = (slot_index < tile_count).astype(jnp.float32)
        place_matrix = (target_index[:, None] == target_part[None, :]).astype(
            jnp.float32
        ) * live_mask[None, :]
        placed = jnp.dot(
            place_matrix,
            products.reshape(slot_group, tile_size * feat_width),
            precision=lax.Precision.HIGH,
            preferred_element_type=jnp.float32,
        )
        return totals + placed

    start_totals = jnp.zeros((out_tiles, tile_size * feat_width), jnp.float32)
    totals = lax.fori_loop(0, loop_turns, advance, start_totals)
    return totals.reshape(out_tiles, tile_size, feat_width)


def local(features, weight, cotangent, tiles, tile_rows, tile_cols, tile_counts):
    blocks = tiles[0, 0]
    row_ids = tile_rows[0, 0]
    col_ids = tile_cols[0, 0]
    tile_count = tile_counts[0, 0]
    rows_dev, feat_width = features.shape
    slot_count = blocks.shape[0]
    tile_size = blocks.shape[1]
    slot_group = math.gcd(slot_count, 64)
    loop_turns = slot_count // slot_group
    projected = jnp.dot(features, weight, preferred_element_type=jnp.float32).astype(jnp.bfloat16)
    column_set = lax.all_gather(projected, "gr", axis=0, tiled=True)
    column_table = column_set.reshape(-1, tile_size, feat_width)
    row_tiles = lax.axis_size("gc") * rows_dev // tile_size
    partial_rows = tile_pass(
        blocks, col_ids, row_ids, tile_count, column_table, row_tiles, False, loop_turns, slot_group
    ).reshape(-1, feat_width)
    summed = lax.psum_scatter(partial_rows, "gc", scatter_dimension=0, tiled=True)
    gelu_value, gelu_slope = gelu_pair(summed)
    grad_own = (cotangent.astype(jnp.float32) * gelu_slope).astype(jnp.bfloat16)
    grad_rows = lax.all_gather(grad_own, "gc", axis=0, tiled=True)
    output = gelu_value.astype(jnp.bfloat16)
    row_table = grad_rows.reshape(-1, tile_size, feat_width)
    col_tiles = lax.axis_size("gr") * rows_dev // tile_size
    partial_cols = tile_pass(
        blocks, row_ids, col_ids, tile_count, row_table, col_tiles, True, loop_turns, slot_group
    ).reshape(-1, feat_width)
    grad_hidden = lax.psum_scatter(partial_cols, "gr", scatter_dimension=0, tiled=True).astype(
        jnp.bfloat16
    )
    grad_features = lax.dot_general(
        grad_hidden, weight, (((1,), (1,)), ((), ())), preferred_element_type=jnp.float32
    ).astype(jnp.bfloat16)
    local_weight = lax.dot_general(
        features, grad_hidden, (((0,), (0,)), ((), ())), preferred_element_type=jnp.float32
    )
    node_total = rows_dev * lax.axis_size("gr") * lax.axis_size("gc")
    grad_weight = lax.psum(local_weight, ("gr", "gc")) / math.sqrt(node_total)
    return (output, grad_features, grad_weight)


def solution(mesh):
    return jax.shard_map(
        local,
        mesh=mesh,
        in_specs=(
            P(("gr", "gc"), None),
            P(),
            P(("gr", "gc"), None),
            P("gr", "gc", None, None, None),
            P("gr", "gc", None),
            P("gr", "gc", None),
            P("gr", "gc"),
        ),
        out_specs=(P(("gr", "gc"), None), P(("gr", "gc"), None), P()),
        check_vma=False,
    )
```

profile of v0, /device:TPU:0, one launch (start us, length us, event | category | flops | bytes accessed | tf_op | source)
XLA Modules:
  0.0 837.1 jit_solution(9143674481040660034)
XLA Ops:
  11.1 35.9 %all-gather.3.cloned.1.call-done = bf16[8192,128]{1,0:T(8,128)(2,1)} async-done(((bf16[512,128]{1,0:T(8,128)(2,1)}), bf16[8192,128]{1,0:T(8,128)(2,1)}) %all-gather.3.cloned.1.call-update) | async-done | bytes 2097168 | tf_op jit(solution)/shard_map/all_gather | solution.py:77
  49.8 180.7 %while.28 = (s32[]{:T(128)}, f32[32,16384]{1,0:T(8,128)}, s32[736]{0:T(1024)S(1)}, s32[]{:T(128)}, bf16[736,128,128]{2,1,0:T(8,128)(2,1)}, /*index=5*/s32[736]{0...) while((s32[]{:T(128)}, f32[32,16384]{1,0:T(8,128)}, ...), condition=%wide.region_1.0_spmd.clone, body=%wide.region_0.0_spmd.clone.sunk | while | flops 303566944 | bytes 32507128 | solution.py:62
  61.2 3.1 convolution_add_fusion.4
  69.0 3.1 convolution_add_fusion.4
  76.9 3.1 convolution_add_fusion.4
  84.7 3.1 convolution_add_fusion.4
  92.6 3.1 convolution_add_fusion.4
  100.5 3.1 convolution_add_fusion.4
  108.3 3.1 convolution_add_fusion.4
  116.2 3.1 convolution_add_fusion.4
  124.0 3.1 convolution_add_fusion.4
  131.9 3.1 convolution_add_fusion.4
  139.7 3.1 convolution_add_fusion.4
  147.6 3.1 convolution_add_fusion.4
  155.5 3.1 convolution_add_fusion.4
  210.5 3.1 convolution_add_fusion.4
  218.3 3.1 convolution_add_fusion.4
  226.2 3.1 convolution_add_fusion.4
  233.4 75.2 %reduce-scatter.3.cloned.1.call-done = f32[512,128]{1,0:T(8,128)} async-done(((f32[4096,128]{1,0:T(8,128)}), f32[512,128]{1,0:T(8,128)}) %reduce-scatter.3.cloned.1.call-update) | async-done | bytes 262160 | tf_op jit(solution)/shard_map/reduce_scatter | solution.py:83
  310.5 30.5 %copy.10 = bf16[1,1,736,128,128]{3,4,2,1,0:T(8,128)(2,1)} copy(bf16[1,1,736,128,128]{4,3,2,1,0:T(8,128)(2,1)} %bitcast.56) | data formatting | bytes 48234496 | tf_op args[3]
  341.0 16.9 %all-gather.5.cloned.1.call-done = bf16[4096,128]{1,0:T(8,128)(2,1)} async-done(((bf16[512,128]{1,0:T(8,128)(2,1)}), bf16[4096,128]{1,0:T(8,128)(2,1)}) %all-gather.5.cloned.1.call-update) | async-done | bytes 1048592 | tf_op jit(solution)/shard_map/all_gather | solution.py:86
  359.4 255.7 %while.29 = (s32[]{:T(128)}, f32[64,16384]{1,0:T(8,128)}, s32[736]{0:T(1024)S(1)}, s32[]{:T(128)}, bf16[736,128,128]{1,2,0:T(8,128)(2,1)}, /*index=5*/s32[736]{0...) while((s32[]{:T(128)}, f32[64,16384]{1,0:T(8,128)}, ...), condition=%wide.region_4.0_spmd.clone, body=%wide.region_3.0_spmd.clone.sunk | while | flops 371725408 | bytes 52430068 | solution.py:62
  363.5 5.0 convolution_add_fusion.5
  374.6 5.0 convolution_add_fusion.5
  385.7 5.0 convolution_add_fusion.5
  396.8 5.0 convolution_add_fusion.5
  408.0 5.0 convolution_add_fusion.5
  419.1 5.0 convolution_add_fusion.5
  430.2 5.0 convolution_add_fusion.5
  441.3 5.0 convolution_add_fusion.5
  452.4 5.0 convolution_add_fusion.5
  463.5 5.0 convolution_add_fusion.5
  474.7 5.0 convolution_add_fusion.5
  485.8 5.0 convolution_add_fusion.5
  496.9 5.0 convolution_add_fusion.5
  508.0 5.0 convolution_add_fusion.5
  519.1 5.0 convolution_add_fusion.5
  530.2 5.0 convolution_add_fusion.5
  541.4 5.0 convolution_add_fusion.5
  552.5 5.0 convolution_add_fusion.5
  563.6 5.0 convolution_add_fusion.5
  574.7 5.0 convolution_add_fusion.5
  585.8 5.0 convolution_add_fusion.5
  596.9 5.0 convolution_add_fusion.5
  608.0 5.0 convolution_add_fusion.5
  615.1 4.9 reshape_reshape.15
  620.1 69.2 %reduce-scatter.5.cloned.1.call-done = f32[512,128]{1,0:T(8,128)} async-done(((f32[8192,128]{1,0:T(8,128)}), f32[512,128]{1,0:T(8,128)}) %reduce-scatter.5.cloned.1.call-update) | async-done | bytes 262160 | tf_op jit(solution)/shard_map/reduce_scatter | solution.py:93
  693.0 136.1 %all-reduce.2.cloned.1.call-done = f32[128,128]{0,1:T(8,128)} async-done(((f32[128,128]{0,1:T(8,128)}), f32[128,128]{0,1:T(8,128)}) %all-reduce.2.cloned.1.call-update) | async-done | bytes 65552 | tf_op jit(solution)/shard_map/psum | solution.py:103
  (496 shorter events, 288.2 us)
Async XLA Ops:
  7.2 39.8 %all-gather.3.cloned.1.call-start = ((), (), s32[]{:S(2)}) async-start(), calls=%async_computation.2 | async-start | bytes 2228224 | tf_op jit(solution)/shard_map/all_gather | solution.py:77
  9.7 298.9 %reduce-scatter.3.cloned.1.call-start = ((), (), s32[]{:S(2)}) async-start(), calls=%async_computation.3 | async-start | bytes 2359296 | tf_op jit(solution)/shard_map/reduce_scatter | solution.py:83
  233.3 75.3 %copy-start.5 = (bf16[512,128]{1,0:T(8,128)(2,1)S(1)}, bf16[512,128]{1,0:T(8,128)(2,1)}, u32[]{:S(2)}) copy-start(bf16[512,128]{1,0:T(8,128)(2,1)} %param.13) | copy-start | bytes 393220
  233.3 124.6 %all-gather.5.cloned.1.call-start = ((), (), s32[]{:S(2)}) async-start(), calls=%async_computation.4 | async-start | bytes 1179648 | tf_op jit(solution)/shard_map/all_gather | solution.py:86
  310.4 378.9 %reduce-scatter.5.cloned.1.call-start = ((), (), s32[]{:S(2)}) async-start(), calls=%async_computation.5 | async-start | bytes 4456448 | tf_op jit(solution)/shard_map/reduce_scatter | solution.py:93
  361.0 2.5 copy-start.1
  368.5 2.1 copy-start.2
  372.1 2.5 copy-start.1
  379.6 2.1 copy-start.2
  383.2 2.5 copy-start.1
  390.7 2.1 copy-start.2
  394.3 2.5 copy-start.1
  401.9 2.1 copy-start.2
  405.5 2.5 copy-start.1
  413.0 2.1 copy-start.2
  416.6 2.5 copy-start.1
  424.1 2.1 copy-start.2
  427.7 2.5 copy-start.1
  435.2 2.1 copy-start.2
  438.8 2.5 copy-start.1
  446.3 2.1 copy-start.2
  449.9 2.5 copy-start.1
  457.4 2.1 copy-start.2
  461.0 2.5 copy-start.1
  468.6 2.1 copy-start.2
  472.1 2.5 copy-start.1
  479.7 2.1 copy-start.2
  483.3 2.5 copy-start.1
  490.8 2.1 copy-start.2
  494.4 2.5 copy-start.1
  501.9 2.1 copy-start.2
  505.5 2.5 copy-start.1
  513.0 2.1 copy-start.2
  516.6 2.5 copy-start.1
  524.1 2.1 copy-start.2
  527.7 2.5 copy-start.1
  535.2 2.1 copy-start.2
  538.8 2.5 copy-start.1
  546.4 2.1 copy-start.2
  550.0 2.5 copy-start.1
  561.1 2.5 copy-start.1
  572.2 2.5 copy-start.1
  583.3 2.5 copy-start.1
  594.4 2.5 copy-start.1
  605.5 2.5 copy-start.1
  613.1 2.1 copy-start.2
  620.0 71.1 %copy-start.6 = (bf16[128,128]{1,0:T(8,128)(2,1)S(1)}, bf16[128,128]{1,0:T(8,128)(2,1)}, u32[]{:S(2)}) copy-start(bf16[128,128]{1,0:T(8,128)(2,1)} %param.12) | copy-start | bytes 98308
  620.0 209.0 %all-reduce.2.cloned.1.call-start = ((), (), s32[]{:S(2)}) async-start(), calls=%async_computation.6 | async-start | bytes 131072 | tf_op jit(solution)/shard_map/psum | solution.py:103
  (52 other events, 85.9 us)
Sparse Core Ops, SparseCore 0:
  10.3 36.6 all-gather.2
  233.4 75.0 reduce-scatter.2
  311.8 46.0 all-gather.4
  620.2 69.1 reduce-scatter.4
  695.2 133.7 all-reduce.1
where the time goes:
time: 842 us; the launch traced here: 837 us
  waiting for transfers between devices  333 us (40%)
  matrix products  296 us (35%)
  local copies, waits for them, and re-layouts  158 us (19%)
  other arithmetic  33.9 us (4%)
  between operations  13.8 us (2%)
    dot_general x46, matrix products, advance(): jnp.dot(place_matrix, products.reshape(slot_group, tile_size * feat_width...  185 us
    psum x1, waiting for transfers between devices, local(): grad_weight = lax.psum(local_weight, ('gr', 'gc')) / math.sqrt(node_total)  136 us
    while x230, local copies, waits for them, and re-layouts  107 us
    reduce_scatter x1, waiting for transfers between devices, local(): lax.psum_scatter(partial_rows, 'gc', scatter_dimension=0, tiled=True)  75.2 us
    reduce_scatter x1, waiting for transfers between devices, local(): lax.psum_scatter(partial_cols, 'gr', scatter_dimension=0, tiled=True)  69.2 us
    dot_general x23, matrix products, advance(): jnp.einsum('sab,saf->sbf', tile_block, picked, preferred_element_type=jnp...  41.6 us
    dot_general x23, matrix products, advance(): jnp.einsum('sab,sbf->saf', tile_block, picked, preferred_element_type=jnp...  41.5 us
    all_gather x1, waiting for transfers between devices, local(): column_set = lax.all_gather(projected, 'gr', axis=0, tiled=True)  35.9 us
  transfers between devices with their start and end apart: 5, of which 5 were waited for; matrix products, arithmetic and copies ran while one was open for 4% of the time, Pallas kernels for 0%

commit v1 on v0

v1 whole, which is shorter than its diff:
```python
import functools
import math

import jax
import jax.numpy as jnp
from jax import lax
from jax.experimental import pallas as pl
from jax.experimental.pallas import tpu as pltpu
from jax.sharding import PartitionSpec as P

TS = 128
F32 = jnp.float32
BF16 = jnp.bfloat16
LAG = 2
MIB = 2**20
VMEM_LIMIT = 8 * MIB

ORDER = (
    [(f, 2, t) for f in (1, 0) for t in (0, 1)]
    + [(f, 1, t) for f in (1, 0) for t in (2, 3)]
    + [(f, 2, t) for f in (1, 0) for t in (2, 3)]
    + [(f, 3, t) for f in (1, 0) for t in (0, 1)]
    + [(f, 1, t) for f in (1, 0) for t in (0, 1)]
    + [(f, 3, t) for f in (1, 0) for t in (2, 3)]
    + [(f, 0, t) for f in (1, 0) for t in range(4)]
)
ARRIVAL = [(f, r, t) for r in (0, 1, 3, 2) for f in (0, 1) for t in range(4)]


def places(order):
    at = [0] * 32
    for i, (far, ring, tile) in enumerate(order):
        at[far * 16 + ring * 4 + tile] = i
    return at


def look_up(index, entries):
    total = jnp.zeros_like(index)
    for at, value in enumerate(entries):
        total = jnp.where(index == at, value, total)
    return total


def group_plan(keys, others, live, cuts, pad, unroll, pad_tile):
    n = keys.shape[0]
    n_keys, n_phases = cuts[-1], len(cuts) - 1
    pad_bits, turn_bits = pad.bit_length() - 1, unroll.bit_length() - 1
    key = jnp.where(live, keys, n_keys)
    slot = jnp.arange(n, dtype=jnp.int32)
    before = (key[:, None] == key[None, :]) & (slot[None, :] < slot[:, None])
    rank = jnp.sum(before.astype(jnp.int32), axis=1)
    every = jnp.arange(n_keys, dtype=jnp.int32)
    counts = jnp.sum((key[None, :] == every[:, None]).astype(jnp.int32), axis=1)
    groups = (counts + pad - 1) >> pad_bits
    phase = jnp.zeros_like(every)
    for cut in cuts[1:-1]:
        phase = phase + (every >= cut).astype(jnp.int32)
    phases = jnp.arange(n_phases, dtype=jnp.int32)
    held = jnp.sum(jnp.where(phase[None, :] == phases[:, None], groups[None, :], 0), axis=1)
    turns = (held + unroll - 1) >> turn_bits
    edges = jnp.arange(n_phases + 1, dtype=jnp.int32)
    bounds = jnp.sum(jnp.where(phases[None, :] < edges[:, None], turns[None, :], 0), axis=1)
    earlier = jnp.where(phases[None, :] < phase[:, None], turns[None, :] << turn_bits, 0)
    ahead = (phase[None, :] == phase[:, None]) & (every[None, :] < every[:, None])
    starts = jnp.sum(jnp.where(ahead, groups[None, :], 0), axis=1) + jnp.sum(earlier, axis=1)
    first = jnp.sum(jnp.where(key[:, None] == every[None, :], starts[None, :], 0), axis=1)
    place = jnp.where(live, (first << pad_bits) + rank, -1)
    most = (n + (pad - 1) * n_keys) // pad + n_phases * (unroll - 1)
    most = -(-most // unroll) * unroll
    spot = jnp.arange(most * pad, dtype=jnp.int32)
    hit = place[None, :] == spot[:, None]
    code = jnp.sum(jnp.where(hit, ((slot << 7) + others - pad_tile)[None, :], 0), axis=1) + pad_tile
    turn = jnp.arange(most, dtype=jnp.int32)
    group_key = jnp.sum((starts[None, :] <= turn[:, None]).astype(jnp.int32), axis=1) - 1
    return bounds, code >> 7, code & 127, group_key


def group_kernel(
    table_cuts, table_size, phase, first_key, pad, unroll, forward, n_extra, finish, *refs
):
    bounds_ref, tile_ref, other_ref, key_ref, tiles_ref = refs[:5]
    n_tables = len(table_cuts)
    table_refs = refs[5 : 5 + n_tables]
    extra_refs = refs[5 + n_tables : 5 + n_tables + n_extra]
    out_refs = refs[5 + n_tables + n_extra : -2]
    table, acc = refs[-2:]
    for ref, (at, start, size) in zip(table_refs, table_cuts):
        table[at : at + size] = ref[start : start + size]
    table[table_size] = jnp.zeros((TS, TS), table.dtype)
    acc[...] = jnp.zeros_like(acc)

    def product(group):
        picked = [tiles_ref[tile_ref[group * pad + i]] for i in range(pad)]
        rest = [table[other_ref[group * pad + i]] for i in range(pad)]
        if forward:
            left, right = picked, rest
        else:
            left, right = rest, picked
        return jnp.dot(
            jnp.concatenate(left, 1), jnp.concatenate(right, 0), preferred_element_type=F32
        )

    @pl.loop(bounds_ref[phase], bounds_ref[phase + 1])
    def _(turn):
        waiting = []
        for i in range(unroll):
            waiting.append((key_ref[turn * unroll + i] - first_key, product(turn * unroll + i)))
            if len(waiting) > LAG:
                key, value = waiting.pop(0)
                acc[key] += value
        for key, value in waiting:
            acc[key] += value

    finish(acc, extra_refs, out_refs)


def group_pass(
    plan, tiles, tables, table_size, phase, keys, pad, unroll, forward, extras, outs, finish, name
):
    bounds, tile_at, other_at, key_at = plan
    scalar = pl.BlockSpec(memory_space=pltpu.SMEM)
    here = pl.BlockSpec(memory_space=pltpu.VMEM)
    n_keys = keys[1] - keys[0]
    share = tiles.shape[0] * n_keys // 64 if forward else tiles.shape[0] * n_keys // 96
    return pl.pallas_call(
        functools.partial(
            group_kernel,
            tuple(t[1:] for t in tables),
            table_size,
            phase,
            keys[0],
            pad,
            unroll,
            forward,
            len(extras),
            finish,
        ),
        out_shape=outs,
        in_specs=[scalar] * 4 + [here] * (1 + len(tables) + len(extras)),
        out_specs=[here] * len(outs),
        scratch_shapes=[
            pltpu.VMEM((table_size + 1, TS, TS), BF16),
            pltpu.VMEM((n_keys, TS, TS), F32),
        ],
        compiler_params=pltpu.CompilerParams(vmem_limit_bytes=VMEM_LIMIT),
        cost_estimate=pl.CostEstimate(
            flops=2 * share * TS**3 * 8, bytes_accessed=4 * MIB, transcendentals=0
        ),
        name=name,
    )(bounds, tile_at, other_at, key_at, tiles, *[t[0] for t in tables], *extras)


def array(tiles, dtype=BF16):
    return jax.ShapeDtypeStruct((tiles, TS, TS), dtype)


def write_parts(acc, extra_refs, out_refs):
    del extra_refs
    at = 0
    for ref in out_refs:
        size = ref.shape[0]
        ref[...] = acc[at : at + size].astype(ref.dtype)
        at += size


def finish_early(acc, extra_refs, out_refs):
    del extra_refs
    out_refs[0][...] = acc[...]


def finish_theirs(acc, extra_refs, out_refs):
    early, own, following, previous, opposite = extra_refs
    theirs, weight_part = out_refs
    theirs[0:32] = (acc[...] + early[...]).astype(BF16)
    across = own[8].astype(F32) + opposite[4].astype(F32)
    beside = following[8].astype(F32) + previous[8].astype(F32)
    total = (across + beside).astype(BF16)
    theirs[32] = total
    weight_part[0] = total


def finish_mine(acc, extra_refs, out_refs):
    (got,) = extra_refs
    plus2, minus2, keep_far, keep = out_refs
    plus2[0:4] = (acc[0:4] + got[16:20].astype(F32)).astype(BF16)
    plus2[4] = jnp.zeros((TS, TS), BF16)
    minus2[...] = (acc[4:8] + got[20:24].astype(F32)).astype(BF16)
    keep_far[...] = acc[8:12] + got[24:28].astype(F32)
    keep[...] = acc[12:16] + got[28:32].astype(F32)


def call(kernel, outs, name, tiles, *args):
    return pl.pallas_call(
        lambda tiles_ref, *refs: kernel(*refs),
        out_shape=outs,
        compiler_params=pltpu.CompilerParams(vmem_limit_bytes=VMEM_LIMIT),
        name=name,
    )(tiles, *args)


def gelu_pair(pre_act):
    coeff = 0.7978845608028654
    cubed = pre_act * pre_act * pre_act
    tanh_val = jnp.tanh(coeff * (pre_act + 0.044715 * cubed))
    gelu_value = 0.5 * pre_act * (1.0 + tanh_val)
    gelu_slope = 0.5 * (1.0 + tanh_val) + 0.5 * pre_act * (1.0 - tanh_val * tanh_val) * coeff * (
        1.0 + 3.0 * 0.044715 * pre_act * pre_act
    )
    return (gelu_value, gelu_slope)


def own_sum(keep, plus, minus, plus2, minus2, far, skip):
    at = 4 + skip + (0 if far else 2)
    to = 0 if far else 2
    first = keep[0:2].astype(F32) + minus[at : at + 2].astype(F32) + plus2[to : to + 2].astype(F32)
    second = keep[2:4].astype(F32) + plus[at : at + 2].astype(F32) + minus2[to : to + 2].astype(F32)
    return jnp.concatenate([first, second], 0)


def sums_kernel(keep_far, keep, plus, minus, plus2, minus2, out_ref):
    out_ref[0:4] = own_sum(keep, plus, minus, plus2, minus2, False, 0).astype(BF16)
    out_ref[4:8] = own_sum(keep_far, plus, minus, plus2, minus2, True, 0).astype(BF16)


def middle_kernel(mine, got, weight, cotangent, far_cotangent, out_ref, pair_ref):
    w = weight[...]
    terms = []
    for at, block_cotangent in ((0, cotangent), (4, far_cotangent)):
        sums = mine[at : at + 4].astype(F32) + got[4 - at : 8 - at].astype(F32)
        mixed = sums.reshape(4 * TS, TS)
        high = mixed.astype(BF16)
        low = (mixed - high.astype(F32)).astype(BF16)
        pre_act = jnp.dot(high, w, preferred_element_type=F32) + jnp.dot(
            low, w, preferred_element_type=F32
        )
        value, slope = gelu_pair(pre_act)
        if at == 0:
            out_ref[...] = value.astype(BF16)
        grad_pre = (block_cotangent[...].astype(F32) * slope).astype(BF16)
        for i in range(4):
            pair_ref[at + i] = lax.dot_general(
                w,
                grad_pre[i * TS : (i + 1) * TS],
                (((1,), (1,)), ((), ())),
                preferred_element_type=F32,
            ).astype(BF16)
        terms.append(
            lax.dot_general(
                high, grad_pre, (((0,), (0,)), ((), ())), preferred_element_type=F32
            )
        )
    pair_ref[8] = (terms[0] + terms[1]).astype(BF16)


def join_kernel(*refs):
    at = 0
    for ref in refs[:-1]:
        refs[-1][at : at + ref.shape[0]] = ref[...]
        at += ref.shape[0]


def add_core_kernel(mine, got, weight_part, plus, minus):
    weight_sum = (weight_part[0].astype(F32) + got[32].astype(F32)).astype(BF16)
    for at, ref in ((0, plus), (8, minus)):
        total = (mine[at : at + 8].astype(F32) + got[at : at + 8].astype(F32)).astype(BF16)
        ref[0:4] = total[0:4]
        ref[4] = weight_sum
        ref[5:9] = total[4:8]


def far_weight_kernel(keep, plus, minus, plus2, minus2, own_plus, out_ref):
    out_ref[0:4] = own_sum(keep, plus, minus, plus2, minus2, True, 1).astype(BF16)
    across = own_plus[4].astype(F32) + plus2[4].astype(F32)
    beside = plus[4].astype(F32) + minus[4].astype(F32)
    out_ref[4] = (across + beside).astype(BF16)


def last_kernel(scale, keep, plus, minus, plus2, minus2, own_far, got_far, grad_ref, weight_ref):
    total = own_sum(keep, plus, minus, plus2, minus2, False, 1) + got_far[0:4].astype(F32)
    for i in range(4):
        grad_ref[i * TS : (i + 1) * TS] = jnp.transpose(total[i]).astype(BF16)
    weight_ref[...] = (own_far[4].astype(F32) + got_far[4].astype(F32)) * scale


def ring_permutes(axis):
    if axis == "gr":
        up = [(i, (i + 4) % 16) for i in range(16)]
    else:
        up = [(i, (i & 4) | ((i + 1) & 3)) for i in range(8)]
    down = [(j, i) for i, j in up]
    return lambda v: lax.ppermute(v, axis, up), lambda v: lax.ppermute(v, axis, down)


def pair_permute(axis, mask):
    size = {"gr": 16, "gc": 8}[axis]
    return lambda value: lax.ppermute(value, axis, [(i, i ^ mask) for i in range(size)])


def local(features, weight, cotangent, tiles, tile_rows, tile_cols, tile_counts):
    gr, gc = lax.axis_index("gr"), lax.axis_index("gc")
    rows, cols = tile_rows[0, 0], tile_cols[0, 0]
    live = jnp.arange(rows.shape[0], dtype=jnp.int32) < tile_counts[0, 0]
    sent, arrived = places(ORDER), places(ARRIVAL)

    owner = rows >> 2
    row_at = (((owner ^ gc) >> 2) & 1) * 16 + ((owner - gc) & 3) * 4 + (rows & 3)
    row_sent, row_arrived = look_up(row_at, sent), look_up(row_at, arrived)
    holder = cols >> 2
    core = (holder ^ gr) & 1
    col_at = (((holder ^ gr) >> 1) & 1) * 16 + (((holder >> 2) - (gr >> 2)) & 3) * 4 + (cols & 3)
    col_sent, col_arrived = look_up(col_at, sent), look_up(col_at, arrived)
    forward_plan = group_plan(row_sent, core * 32 + col_arrived, live, (0, 16, 32), 4, 16, 64)
    theirs_key = jnp.where(row_arrived < 24, 0, 32) + col_sent
    back_key = jnp.where(core == 1, theirs_key, 64 + col_sent)
    backward_plan = group_plan(back_key, row_arrived, live, (0, 32, 64, 80, 96), 2, 16, 32)

    core_swap, y_swap = pair_permute("gr", 1), pair_permute("gr", 2)
    w_swap = pair_permute("gc", 4)
    z_up, z_down = ring_permutes("gr")
    x_up, x_down = ring_permutes("gc")

    own = features.reshape(4, TS, TS)
    far = y_swap(own)
    pair = jnp.concatenate([own, far], 0)
    previous, following = z_up(pair), z_down(pair)
    blocks = pltpu.with_memory_space_constraint(tiles[0, 0], pltpu.VMEM)
    held = call(join_kernel, array(8), "after_tiles", blocks, pair)
    near = call(join_kernel, array(24), "near_columns", blocks, held, following, previous)
    opposite = call(
        join_kernel, array(8), "opposite_columns",
        blocks, z_up(previous[:4]), z_down(following[4:8]),
    )
    tables = [
        (near, 0, 0, 24),
        (opposite, 24, 0, 8),
        (core_swap(near), 32, 0, 24),
        (core_swap(opposite), 56, 0, 8),
    ]
    plus, minus = group_pass(
        forward_plan, blocks, tables, 64, 0, (0, 16), 4, 16, True, [], [array(8)] * 2, write_parts,
        "forward_sent",
    )

    got_plus, got_minus = x_up(plus), x_down(minus)
    plus2, minus2, keep_far, keep = group_pass(
        forward_plan, blocks, tables, 64, 1, (16, 32), 4, 16, True, [],
        [array(4), array(4), array(4, F32), array(4, F32)], write_parts, "forward_kept",
    )
    got_plus2 = x_up((plus2.astype(F32) + got_plus[:4].astype(F32)).astype(BF16))
    got_minus2 = x_down((minus2.astype(F32) + got_minus[:4].astype(F32)).astype(BF16))
    got = (got_plus, got_minus, got_plus2, got_minus2)
    sums = call(sums_kernel, array(8), "row_sums", blocks, keep_far, keep, *got)
    output, pair = call(
        middle_kernel,
        [jax.ShapeDtypeStruct(cotangent.shape, BF16), array(9)],
        "middle",
        blocks, sums, w_swap(sums), weight, cotangent, w_swap(cotangent),
    )

    previous, following = x_up(pair), x_down(pair)
    opposite_near, opposite_far = x_up(previous[:4]), x_down(following[4:9])
    early = [(pair, 0, 0, 8), (following, 8, 0, 8), (previous, 16, 0, 8)]
    late = [(opposite_near, 24, 0, 4), (opposite_far, 28, 0, 4)]
    (sums,) = group_pass(
        backward_plan, blocks, early, 32, 0, (0, 32), 2, 16, False, [], [array(32, F32)],
        finish_early, "backward_early",
    )
    theirs, weight_part = group_pass(
        backward_plan, blocks, late, 32, 1, (32, 64), 2, 16, False,
        [sums, pair, following, previous, opposite_far], [array(33), array(1)],
        finish_theirs, "backward_theirs",
    )

    got = core_swap(theirs)
    (mine,) = group_pass(
        backward_plan, blocks, early + late, 32, 2, (64, 80), 2, 16, False, [], [array(16)],
        write_parts, "backward_sent",
    )
    plus, minus = call(add_core_kernel, [array(9)] * 2, "add_core", blocks, mine, got, weight_part)
    got_plus, got_minus = z_up(plus), z_down(minus)
    plus2, minus2, keep_far, keep = group_pass(
        backward_plan, blocks, early + late, 32, 3, (80, 96), 2, 16, False, [got],
        [array(5), array(4), array(4, F32), array(4, F32)], finish_mine, "backward_kept",
    )
    got_plus2 = z_up((plus2.astype(F32) + got_plus[:5].astype(F32)).astype(BF16))
    got_minus2 = z_down((minus2.astype(F32) + got_minus[:4].astype(F32)).astype(BF16))
    got = (got_plus, got_minus, got_plus2, got_minus2)
    far = call(far_weight_kernel, array(5), "far_columns", blocks, keep_far, *got, plus)
    nodes = features.shape[0] * lax.axis_size("gr") * lax.axis_size("gc")
    grad_features, grad_weight = call(
        functools.partial(last_kernel, 1.0 / math.sqrt(nodes)),
        [jax.ShapeDtypeStruct(features.shape, BF16), jax.ShapeDtypeStruct((TS, TS), F32)],
        "last",
        blocks, keep, *got, far, y_swap(far),
    )
    return (output, grad_features, grad_weight)


def solution(mesh):
    return jax.shard_map(
        local,
        mesh=mesh,
        in_specs=(
            P(("gr", "gc"), None),
            P(),
            P(("gr", "gc"), None),
            P("gr", "gc", None, None, None),
            P("gr", "gc", None),
            P("gr", "gc", None),
            P("gr", "gc"),
        ),
        out_specs=(P(("gr", "gc"), None), P(("gr", "gc"), None), P()),
        check_vma=False,
    )
```

time: 842 us -> 113 us (0.13)
  matrix products: 296 us -> 0 us
  waiting for transfers between devices: 333 us -> 37.3 us
  local copies, waits for them, and re-layouts: 158 us -> 7.94 us
  starting transfers between devices: 0.21 us -> 39.4 us
  other arithmetic: 33.9 us -> 6.89 us
  Pallas kernels: 0 us -> 17.5 us
  between operations: 13.8 us -> 1.75 us
    dot_general x141 -> x0, matrix products: 296 us -> none  [the longest x46 185 us: advance(): jnp.dot(place_matrix, products.reshape(slot_group, tile_size * feat_width...]
    reduce_scatter x2 -> x0, waiting for transfers between devices: 144 us -> none  [the longest x1 75.2 us: local(): lax.psum_scatter(partial_rows, 'gc', scatter_dimension=0, tiled=True)]
    psum x1 -> x0, waiting for transfers between devices: 136 us -> none  [local(): grad_weight = lax.psum(local_weight, ('gr', 'gc')) / math.sqrt(node_total)]
    while x230 -> x0, local copies, waits for them, and re-layouts: 107 us -> none
    all_gather x2 -> x0, waiting for transfers between devices: 52.7 us -> none  [the longest x1 35.9 us: local(): column_set = lax.all_gather(projected, 'gr', axis=0, tiled=True)]
    ppermute x0 -> x23, starting transfers between devices: none -> 39.4 us  [the longest x8 17.8 us: ring_permutes(): lax.ppermute(v, axis, down)]
    ppermute x0 -> x23, waiting for transfers between devices: none -> 37.3 us  [the longest x8 22.3 us: ring_permutes(): lax.ppermute(v, axis, up)]
    convert_element_type x47 -> x5, other arithmetic: 31.7 us -> 0.16 us  [the longest x2 0.08 us: local(): (minus2.astype(F32) + got_minus[:4].astype(F32)).astype(BF16)]
  transfers between devices with their start and end apart: 5 -> 23, of which waited for: 5 -> 12; matrix products, arithmetic and copies ran while one was open for 4% -> 5% of each run, Pallas kernels for 0% -> 9%
where the time goes in v1:
time: 113 us; the launch traced here: 111 us
  starting transfers between devices  39.4 us (35%)
  waiting for transfers between devices  37.3 us (33%)
  Pallas kernels  17.5 us (15%)
  local copies, waits for them, and re-layouts  7.94 us (7%)
  other arithmetic  6.89 us (6%)
  between operations  1.75 us (2%)
    ppermute x8, waiting for transfers between devices, ring_permutes(): lax.ppermute(v, axis, up)  22.3 us
    ppermute x8, starting transfers between devices, ring_permutes(): lax.ppermute(v, axis, down)  17.8 us
    pallas_call x6, Pallas kernels, group_pass(): pl.pallas_call(functools.partial(group_kernel, tuple((t[1:] for t in tabl...  15.1 us
    ppermute x7, waiting for transfers between devices, pair_permute(): lax.ppermute(value, axis, [(i, i ^ mask) for i in range(size)])  12.4 us
    ppermute x8, starting transfers between devices, ring_permutes(): lax.ppermute(v, axis, up)  11 us
    ppermute x7, starting transfers between devices, pair_permute(): lax.ppermute(value, axis, [(i, i ^ mask) for i in range(size)])  10.6 us
    unnamed x18, local copies, waits for them, and re-layouts  7.89 us
    ppermute x8, waiting for transfers between devices, ring_permutes(): lax.ppermute(v, axis, down)  2.59 us
  transfers between devices with their start and end apart: 23, of which 12 were waited for; matrix products, arithmetic and copies ran while one was open for 5% of the time, Pallas kernels for 9%

profile of v1, /device:TPU:0, one launch (start us, length us, event | category | flops | bytes accessed | tf_op | source)
XLA Modules:
  0.0 110.7 jit_solution(17599309876886736513)
XLA Ops:
  0.6 1.7 %collective-permute-start = (bf16[4,128,128]{2,1,0:T(8,128)(2,1)}, bf16[4,128,128]{2,1,0:T(8,128)(2,1)S(1)}, u32[]{:S(2)}, u32[]{:S(2)}) collective-permute-start(bf16[4,128,128]{2,1,0:T(8,128)(2,1)} %bitcast.22), channel_id=1, source_target_pairs={{0,16},{8,24},{16,0},{24,8},{32,48},{40,56},{48,32},{56,40},{64,80... | collective-permute-start | bytes 393224 | tf_op jit(solution)/shard_map/ppermute | solution.py:296
  2.4 0.7 fusion.4
  3.1 0.2 compare_reduce_fusion.24
  4.0 0.7 compare_reduce_fusion.48
  4.7 0.7 fusion.6
  5.4 0.2 compare_reduce_fusion
  5.7 0.3 convert_reduce_fusion
  6.1 0.1 convert_reduce_fusion.2
  6.2 0.2 select_reduce_fusion.4
  6.7 0.3 convert_reduce_fusion.1
  7.1 0.2 select_reduce_fusion.5
  7.7 0.9 pad_maximum_fusion.refs_0_
  8.7 4.1 %collective-permute-start.1 = (bf16[8,128,128]{2,1,0:T(8,128)(2,1)S(1)}, bf16[8,128,128]{2,1,0:T(8,128)(2,1)S(1)}, u32[]{:S(2)}, u32[]{:S(2)}) collective-permute-start(bf16[8,128,128]{2,1,0:T(8,128)(2,1)S(1)} %pad_maximum_fusion.refs_0_), channel_id=1, source_target_pairs={{32,0},{40,8},{48,16},{56,24},{64,32},{72,40},{80,48},{88,56},{96,... | collective-permute-start | bytes 786440 | tf_op jit(solution)/shard_map/ppermute | solution.py:291
  12.9 7.8 %copy-done = bf16[1,1,736,128,128]{4,3,2,1,0:T(8,128)(2,1)S(1)} copy-done((bf16[1,1,736,128,128]{4,3,2,1,0:T(8,128)(2,1)S(1)}, bf16[1,1,736,128,128]{4,3,2,1,0:T(8,128)(2,1)}, u32[]{:S(2)}) %copy-start) | copy-done | bytes 24117272
  20.8 0.7 collective-permute-done.2.refs_2_
  21.8 3.3 %collective-permute-start.4 = (bf16[4,128,128]{2,1,0:T(8,128)(2,1)S(1)}, bf16[4,128,128]{2,1,0:T(8,128)(2,1)S(1)}, u32[]{:S(2)}, u32[]{:S(2)}) collective-permute-start(bf16[4,128,128]{2,1,0:T(8,128)(2,1)S(1)} %slice.33), channel_id=1, source_target_pairs={{32,0},{40,8},{48,16},{56,24},{64,32},{72,40},{80,48},{88,56},{96,... | collective-permute-start | bytes 393224 | tf_op jit(solution)/shard_map/ppermute | solution.py:291
  25.1 0.4 select_reduce_fusion.1
  25.5 3.4 %collective-permute-done.3.refs_0_ = bf16[4,128,128]{2,1,0:T(8,128)(2,1)S(1)} collective-permute-done((bf16[4,128,128]{2,1,0:T(8,128)(2,1)S(1)}, bf16[4,128,128]{2,1,0:T(8,128)(2,1)S(1)}, u32[]{:S(2)}, u32[]{:S(2)}) %collective-permute-start.3) | collective-permute-done | bytes 131104 | tf_op jit(solution)/shard_map/ppermute | solution.py:291
  29.1 1.4 %collective-permute-done.6.refs_8_ = bf16[8,128,128]{2,1,0:T(8,128)(2,1)S(1)} collective-permute-done((bf16[8,128,128]{2,1,0:T(8,128)(2,1)S(1)}, bf16[8,128,128]{2,1,0:T(8,128)(2,1)S(1)}, u32[]{:S(2)}, u32[]{:S(2)}) %collective-permute-start.6) | collective-permute-done | bytes 262176 | tf_op jit(solution)/shard_map/ppermute | solution.py:296
  30.6 3.1 %forward_sent.1 = (bf16[8,128,128]{2,1,0:T(8,128)(2,1)S(1)}, bf16[8,128,128]{2,1,0:T(8,128)(2,1)S(1)}) custom-call(s32[3]{0:T(128)S(1)} %fusion.8.refs_0_, s32[960]{0:T(1024)S(1)} %get-tuple-element.98.refs_1_, s32[960]{0:T(1024)S(1)} %get-tuple-element.97.refs_2_, s32[240]{0:T(256)S(1)} %broadcast_add_fusion.1.refs_3_, bf16[736,128,128]{2,1,0:T(8,128)(2,1)S(1)} %bitcast.11, ...), custom_call_target="tpu_custom_call" | custom-call | flops 6174015488 | bytes 4194304 | tf_op jit(solution)/shard_map/forward_sent/pallas_call | solution.py:125
  33.6 3.7 %collective-permute-start.7 = (bf16[8,128,128]{2,1,0:T(8,128)(2,1)S(1)}, bf16[8,128,128]{2,1,0:T(8,128)(2,1)S(1)}, u32[]{:S(2)}, u32[]{:S(2)}) collective-permute-start(bf16[8,128,128]{2,1,0:T(8,128)(2,1)S(1)} %get-tuple-element.23), channel_id=1, source_target_pairs={{0,1},{1,2},{2,3},{3,0},{4,5},{5,6},{6,7},{7,4},{8,9},{9,10},{10,1... | collective-permute-start | bytes 786440 | tf_op jit(solution)/shard_map/ppermute | solution.py:291
  37.3 3.1 %forward_kept.1 = (bf16[4,128,128]{2,1,0:T(8,128)(2,1)S(1)}, bf16[4,128,128]{2,1,0:T(8,128)(2,1)S(1)}, f32[4,128,128]{2,1,0:T(8,128)S(1)}, f32[4,128,128]{2,1,0:T(8,128)S(1)}) custom-call(s32[3]{0:T(128)S(1)} %fusion.8.refs_0_, s32[960]{0:T(1024)S(1)} %get-tuple-element.98.refs_1_, s32[960]{0:T(1024)S(1)} %get-tuple-element.97.refs_2_, ...), custom_call_target="tpu_custom_call" | custom-call | flops 6174015488 | bytes 4194304 | tf_op jit(solution)/shard_map/forward_kept/pallas_call | solution.py:125
  40.4 2.9 %collective-permute-done.7.refs_2_ = bf16[8,128,128]{2,1,0:T(8,128)(2,1)S(1)} collective-permute-done((bf16[8,128,128]{2,1,0:T(8,128)(2,1)S(1)}, bf16[8,128,128]{2,1,0:T(8,128)(2,1)S(1)}, u32[]{:S(2)}, u32[]{:S(2)}) %collective-permute-start.7) | collective-permute-done | bytes 262176 | tf_op jit(solution)/shard_map/ppermute | solution.py:291
  43.3 2.0 %collective-permute-start.9 = (bf16[4,128,128]{2,1,0:T(8,128)(2,1)S(1)}, bf16[4,128,128]{2,1,0:T(8,128)(2,1)S(1)}, u32[]{:S(2)}, u32[]{:S(2)}) collective-permute-start(bf16[4,128,128]{2,1,0:T(8,128)(2,1)S(1)} %add_convert_fusion.3), channel_id=1, source_target_pairs={{0,1},{1,2},{2,3},{3,0},{4,5},{5,6},{6,7},{7,4},{8,9},{9,10},{10,1... | collective-permute-start | bytes 393224 | tf_op jit(solution)/shard_map/ppermute | solution.py:291
  45.4 1.3 %collective-permute-start.10 = (bf16[4,128,128]{2,1,0:T(8,128)(2,1)S(1)}, bf16[4,128,128]{2,1,0:T(8,128)(2,1)S(1)}, u32[]{:S(2)}, u32[]{:S(2)}) collective-permute-start(bf16[4,128,128]{2,1,0:T(8,128)(2,1)S(1)} %add_convert_fusion.2), channel_id=1, source_target_pairs={{1,0},{2,1},{3,2},{0,3},{5,4},{6,5},{7,6},{4,7},{9,8},{10,9},{11,1... | collective-permute-start | bytes 393224 | tf_op jit(solution)/shard_map/ppermute | solution.py:291
  46.7 5.7 %collective-permute-start.12 = (bf16[512,128]{1,0:T(8,128)(2,1)S(1)}, bf16[512,128]{1,0:T(8,128)(2,1)S(1)}, u32[]{:S(2)}, u32[]{:S(2)}) collective-permute-start(bf16[512,128]{1,0:T(8,128)(2,1)S(1)} %copy-done.1), channel_id=1, source_target_pairs={{0,4},{1,5},{2,6},{3,7},{4,0},{5,1},{6,2},{7,3},{8,12},{9,13},{10,... | collective-permute-start | bytes 393224 | tf_op jit(solution)/shard_map/ppermute | solution.py:296
  52.6 2.8 %collective-permute-start.11 = (bf16[8,128,128]{2,1,0:T(8,128)(2,1)S(1)}, bf16[8,128,128]{2,1,0:T(8,128)(2,1)S(1)}, u32[]{:S(2)}, u32[]{:S(2)}) collective-permute-start(bf16[8,128,128]{2,1,0:T(8,128)(2,1)S(1)} %row_sums.1.refs_0_), channel_id=1, source_target_pairs={{0,4},{1,5},{2,6},{3,7},{4,0},{5,1},{6,2},{7,3},{8,12},{9,13},{10,... | collective-permute-start | bytes 786440 | tf_op jit(solution)/shard_map/ppermute | solution.py:296
  55.4 0.4 select_reduce_fusion
  55.8 0.3 collective-permute-done.12.refs_4_
  56.1 4.9 %collective-permute-done.11.refs_1_ = bf16[8,128,128]{2,1,0:T(8,128)(2,1)S(1)} collective-permute-done((bf16[8,128,128]{2,1,0:T(8,128)(2,1)S(1)}, bf16[8,128,128]{2,1,0:T(8,128)(2,1)S(1)}, u32[]{:S(2)}, u32[]{:S(2)}) %collective-permute-start.11) | collective-permute-done | bytes 262176 | tf_op jit(solution)/shard_map/ppermute | solution.py:296
  61.0 1.3 %middle.1 = (bf16[512,128]{1,0:T(8,128)(2,1)}, bf16[9,128,128]{2,1,0:T(8,128)(2,1)S(1)}) custom-call(bf16[736,128,128]{2,1,0:T(8,128)(2,1)S(1)} %bitcast.14, bf16[8,128,128]{2,1,0:T(8,128)(2,1)S(1)} %row_sums.1.refs_0_, bf16[8,128,128]{2,1,0:T(8,128)(2,1)S(1)} %collective-permute-done.11.refs_1_, bf16[128,128]{1,0:T(8,128)(2,1)S(1)} %copy-done.2, ...), custom_call_target="tpu_custom_call" | custom-call | tf_op jit(solution)/shard_map/middle/pallas_call | solution.py:193
  62.2 2.1 %collective-permute-start.13 = (bf16[9,128,128]{2,1,0:T(8,128)(2,1)S(1)}, bf16[9,128,128]{2,1,0:T(8,128)(2,1)S(1)}, u32[]{:S(2)}, u32[]{:S(2)}) collective-permute-start(bf16[9,128,128]{2,1,0:T(8,128)(2,1)S(1)} %get-tuple-element.28.refs_5_.refs_8_), channel_id=1, source_target_pairs={{1,0},{2,1},{3,2},{0,3},{5,4},{6,5},{7,6},{4,7},{9,8},{10,9},{11,1... | collective-permute-start | bytes 884744 | tf_op jit(solution)/shard_map/ppermute | solution.py:291
  64.5 8.3 %collective-permute-done.14.refs_7_.refs_10_ = bf16[9,128,128]{2,1,0:T(8,128)(2,1)S(1)} collective-permute-done((bf16[9,128,128]{2,1,0:T(8,128)(2,1)S(1)}, bf16[9,128,128]{2,1,0:T(8,128)(2,1)S(1)}, u32[]{:S(2)}, u32[]{:S(2)}) %collective-permute-start.14) | collective-permute-done | bytes 294944 | tf_op jit(solution)/shard_map/ppermute | solution.py:291
  72.9 3.5 %collective-permute-start.16 = (bf16[5,128,128]{2,1,0:T(8,128)(2,1)S(1)}, bf16[5,128,128]{2,1,0:T(8,128)(2,1)S(1)}, u32[]{:S(2)}, u32[]{:S(2)}) collective-permute-start(bf16[5,128,128]{2,1,0:T(8,128)(2,1)S(1)} %slice.37), channel_id=1, source_target_pairs={{1,0},{2,1},{3,2},{0,3},{5,4},{6,5},{7,6},{4,7},{9,8},{10,9},{11,1... | collective-permute-start | bytes 491528 | tf_op jit(solution)/shard_map/ppermute | solution.py:291
  76.4 2.8 %backward_early.1.refs_7_ = f32[32,128,128]{2,1,0:T(8,128)S(1)} custom-call(s32[5]{0:T(128)S(1)} %select_reduce_fusion.7.refs_0_, s32[960]{0:T(1024)S(1)} %get-tuple-element.96.refs_1_, s32[960]{0:T(1024)S(1)} %get-tuple-element.95.refs_2_, s32[480]{0:T(512)S(1)} %broadcast_add_fusion.refs_3_, bf16[736,128,128]{2,1,0:T(8,128)(2,1)S(1)} %bitcast.15, ...), custom_call_target="tpu_custom_call" | custom-call | flops 8220835840 | bytes 4194304 | tf_op jit(solution)/shard_map/backward_early/pallas_call | solution.py:125
  79.2 2.1 %backward_theirs.1 = (bf16[33,128,128]{2,1,0:T(8,128)(2,1)S(1)}, bf16[1,128,128]{2,1,0:T(8,128)(2,1)S(1)}) custom-call(s32[5]{0:T(128)S(1)} %select_reduce_fusion.7.refs_0_, s32[960]{0:T(1024)S(1)} %get-tuple-element.96.refs_1_, s32[960]{0:T(1024)S(1)} %get-tuple-element.95.refs_2_, s32[480]{0:T(512)S(1)} %broadcast_add_fusion.refs_3_, ...), custom_call_target="tpu_custom_call" | custom-call | flops 8220835840 | bytes 4194304 | tf_op jit(solution)/shard_map/backward_theirs/pallas_call | solution.py:125
  81.4 2.2 %backward_sent.1.refs_0_ = bf16[16,128,128]{2,1,0:T(8,128)(2,1)S(1)} custom-call(s32[5]{0:T(128)S(1)} %select_reduce_fusion.7.refs_0_, s32[960]{0:T(1024)S(1)} %get-tuple-element.96.refs_1_, s32[960]{0:T(1024)S(1)} %get-tuple-element.95.refs_2_, s32[480]{0:T(512)S(1)} %broadcast_add_fusion.refs_3_, bf16[736,128,128]{2,1,0:T(8,128)(2,1)S(1)} %bitcast.17, ...), custom_call_target="tpu_custom_call" | custom-call | flops 4093640704 | bytes 4194304 | tf_op jit(solution)/shard_map/backward_sent/pallas_call | solution.py:125
  83.7 0.5 collective-permute-done.17.refs_10_.refs_1_
  84.1 0.1 add_core.1
  84.3 5.1 %collective-permute-start.18 = (bf16[9,128,128]{2,1,0:T(8,128)(2,1)S(1)}, bf16[9,128,128]{2,1,0:T(8,128)(2,1)S(1)}, u32[]{:S(2)}, u32[]{:S(2)}) collective-permute-start(bf16[9,128,128]{2,1,0:T(8,128)(2,1)S(1)} %get-tuple-element.32.refs_5_), channel_id=1, source_target_pairs={{0,32},{8,40},{16,48},{24,56},{32,64},{40,72},{48,80},{56,88},{64,... | collective-permute-start | bytes 884744 | tf_op jit(solution)/shard_map/ppermute | solution.py:291
  89.3 0.2 collective-permute-start.19
  89.5 1.8 %backward_kept.1 = (bf16[5,128,128]{2,1,0:T(8,128)(2,1)S(1)}, bf16[4,128,128]{2,1,0:T(8,128)(2,1)S(1)}, f32[4,128,128]{2,1,0:T(8,128)S(1)}, f32[4,128,128]{2,1,0:T(8,128)S(1)}) custom-call(s32[5]{0:T(128)S(1)} %select_reduce_fusion.7.refs_0_, s32[960]{0:T(1024)S(1)} %get-tuple-element.96.refs_1_, s32[960]{0:T(1024)S(1)} %get-tuple-element.95.refs_2_, ...), custom_call_target="tpu_custom_call" | custom-call | flops 4093640704 | bytes 4194304 | tf_op jit(solution)/shard_map/backward_kept/pallas_call | solution.py:125
  91.4 5.8 %collective-permute-done.18.refs_1_ = bf16[9,128,128]{2,1,0:T(8,128)(2,1)S(1)} collective-permute-done((bf16[9,128,128]{2,1,0:T(8,128)(2,1)S(1)}, bf16[9,128,128]{2,1,0:T(8,128)(2,1)S(1)}, u32[]{:S(2)}, u32[]{:S(2)}) %collective-permute-start.18) | collective-permute-done | bytes 294944 | tf_op jit(solution)/shard_map/ppermute | solution.py:291
  97.3 3.3 %collective-permute-start.21 = (bf16[4,128,128]{2,1,0:T(8,128)(2,1)S(1)}, bf16[4,128,128]{2,1,0:T(8,128)(2,1)S(1)}, u32[]{:S(2)}, u32[]{:S(2)}) collective-permute-start(bf16[4,128,128]{2,1,0:T(8,128)(2,1)S(1)} %add_convert_fusion.1), channel_id=1, source_target_pairs={{32,0},{40,8},{48,16},{56,24},{64,32},{72,40},{80,48},{88,56},{96,... | collective-permute-start | bytes 393224 | tf_op jit(solution)/shard_map/ppermute | solution.py:291
  100.6 2.6 %collective-permute-done.21.refs_4_ = bf16[4,128,128]{2,1,0:T(8,128)(2,1)S(1)} collective-permute-done((bf16[4,128,128]{2,1,0:T(8,128)(2,1)S(1)}, bf16[4,128,128]{2,1,0:T(8,128)(2,1)S(1)}, u32[]{:S(2)}, u32[]{:S(2)}) %collective-permute-start.21) | collective-permute-done | bytes 131104 | tf_op jit(solution)/shard_map/ppermute | solution.py:291
  103.2 1.3 %collective-permute-done.20.refs_3_ = bf16[5,128,128]{2,1,0:T(8,128)(2,1)S(1)} collective-permute-done((bf16[5,128,128]{2,1,0:T(8,128)(2,1)S(1)}, bf16[5,128,128]{2,1,0:T(8,128)(2,1)S(1)}, u32[]{:S(2)}, u32[]{:S(2)}) %collective-permute-start.20) | collective-permute-done | bytes 163872 | tf_op jit(solution)/shard_map/ppermute | solution.py:291
  104.6 5.3 %collective-permute-done.22.refs_6_ = bf16[5,128,128]{2,1,0:T(8,128)(2,1)S(1)} collective-permute-done((bf16[5,128,128]{2,1,0:T(8,128)(2,1)S(1)}, bf16[5,128,128]{2,1,0:T(8,128)(2,1)S(1)}, u32[]{:S(2)}, u32[]{:S(2)}) %collective-permute-start.22) | collective-permute-done | bytes 163872 | tf_op jit(solution)/shard_map/ppermute | solution.py:296
  109.9 0.8 last.1
  (80 shorter events, 2.4 us)
Async XLA Ops:
  0.6 7.1 %collective-permute-start = (bf16[4,128,128]{2,1,0:T(8,128)(2,1)}, bf16[4,128,128]{2,1,0:T(8,128)(2,1)S(1)}, u32[]{:S(2)}, u32[]{:S(2)}) collective-permute-start(bf16[4,128,128]{2,1,0:T(8,128)(2,1)} %bitcast.22), channel_id=1, source_target_pairs={{0,16},{8,24},{16,0},{24,8},{32,48},{40,56},{48,32},{56,40},{64,80... | collective-permute-start | bytes 393224 | tf_op jit(solution)/shard_map/ppermute | solution.py:296
  8.7 12.1 %collective-permute-start.1 = (bf16[8,128,128]{2,1,0:T(8,128)(2,1)S(1)}, bf16[8,128,128]{2,1,0:T(8,128)(2,1)S(1)}, u32[]{:S(2)}, u32[]{:S(2)}) collective-permute-start(bf16[8,128,128]{2,1,0:T(8,128)(2,1)S(1)} %pad_maximum_fusion.refs_0_), channel_id=1, source_target_pairs={{32,0},{40,8},{48,16},{56,24},{64,32},{72,40},{80,48},{88,56},{96,... | collective-permute-start | bytes 786440 | tf_op jit(solution)/shard_map/ppermute | solution.py:291
  12.8 8.7 %collective-permute-start.2 = (bf16[8,128,128]{2,1,0:T(8,128)(2,1)S(1)}, bf16[8,128,128]{2,1,0:T(8,128)(2,1)S(1)}, u32[]{:S(2)}, u32[]{:S(2)}) collective-permute-start(bf16[8,128,128]{2,1,0:T(8,128)(2,1)S(1)} %pad_maximum_fusion.refs_0_), channel_id=1, source_target_pairs={{0,32},{8,40},{16,48},{24,56},{32,64},{40,72},{48,80},{56,88},{64,... | collective-permute-start | bytes 786440 | tf_op jit(solution)/shard_map/ppermute | solution.py:291
  12.9 7.9 %copy-start = (bf16[1,1,736,128,128]{4,3,2,1,0:T(8,128)(2,1)S(1)}, bf16[1,1,736,128,128]{4,3,2,1,0:T(8,128)(2,1)}, u32[]{:S(2)}) copy-start(bf16[1,1,736,128,128]{4,3,2,1,0:T(8,128)(2,1)} %param.10) | copy-start | bytes 72351744
  20.8 8.1 %slice-start = ((s8[24117248]{0:T(1024)(128)(4,1)}), s8[4194304]{0:T(1024)(128)(4,1)S(1)}, s32[]{:S(2)}) async-start(s8[24117248]{0:T(1024)(128)(4,1)} %bitcast.8), calls=%async_computation | async-start | bytes 8388608
  20.8 8.1 %slice-start.1 = ((s8[24117248]{0:T(1024)(128)(4,1)}), s8[4194304]{0:T(1024)(128)(4,1)S(1)}, s32[]{:S(2)}) async-start(s8[24117248]{0:T(1024)(128)(4,1)} %bitcast.8), calls=%async_computation.1 | async-start | bytes 8388608
  20.8 8.1 %slice-start.2 = ((s8[24117248]{0:T(1024)(128)(4,1)}), s8[4194304]{0:T(1024)(128)(4,1)S(1)}, s32[]{:S(2)}) async-start(s8[24117248]{0:T(1024)(128)(4,1)} %bitcast.8), calls=%async_computation.2 | async-start | bytes 8388608
  20.8 8.1 %slice-start.3 = ((s8[24117248]{0:T(1024)(128)(4,1)}), s8[4194304]{0:T(1024)(128)(4,1)S(1)}, s32[]{:S(2)}) async-start(s8[24117248]{0:T(1024)(128)(4,1)} %bitcast.8), calls=%async_computation.3 | async-start | bytes 8388608
  20.8 8.1 %slice-start.4 = ((s8[24117248]{0:T(1024)(128)(4,1)}), s8[4194304]{0:T(1024)(128)(4,1)S(1)}, s32[]{:S(2)}) async-start(s8[24117248]{0:T(1024)(128)(4,1)} %bitcast.8), calls=%async_computation.4 | async-start | bytes 8388608
  20.8 8.1 %slice-start.5 = ((s8[24117248]{0:T(1024)(128)(4,1)}), s8[3145728]{0:T(1024)(128)(4,1)S(1)}, s32[]{:S(2)}) async-start(s8[24117248]{0:T(1024)(128)(4,1)} %bitcast.8), calls=%async_computation.5 | async-start | bytes 6291456
  21.5 9.0 %collective-permute-start.5 = (bf16[24,128,128]{2,1,0:T(8,128)(2,1)S(1)}, bf16[24,128,128]{2,1,0:T(8,128)(2,1)S(1)}, u32[]{:S(2)}, u32[]{:S(2)}) collective-permute-start(bf16[24,128,128]{2,1,0:T(8,128)(2,1)S(1)} %near_columns.1.refs_5_), channel_id=1, source_target_pairs={{0,8},{8,0},{16,24},{24,16},{32,40},{40,32},{48,56},{56,48},{64,72... | collective-permute-start | bytes 2359304 | tf_op jit(solution)/shard_map/ppermute | solution.py:296
  21.7 7.2 %collective-permute-start.3 = (bf16[4,128,128]{2,1,0:T(8,128)(2,1)S(1)}, bf16[4,128,128]{2,1,0:T(8,128)(2,1)S(1)}, u32[]{:S(2)}, u32[]{:S(2)}) collective-permute-start(bf16[4,128,128]{2,1,0:T(8,128)(2,1)S(1)} %slice.32), channel_id=1, source_target_pairs={{0,32},{8,40},{16,48},{24,56},{32,64},{40,72},{48,80},{56,88},{64,... | collective-permute-start | bytes 393224 | tf_op jit(solution)/shard_map/ppermute | solution.py:291
  21.8 7.1 %collective-permute-start.4 = (bf16[4,128,128]{2,1,0:T(8,128)(2,1)S(1)}, bf16[4,128,128]{2,1,0:T(8,128)(2,1)S(1)}, u32[]{:S(2)}, u32[]{:S(2)}) collective-permute-start(bf16[4,128,128]{2,1,0:T(8,128)(2,1)S(1)} %slice.33), channel_id=1, source_target_pairs={{32,0},{40,8},{48,16},{56,24},{64,32},{72,40},{80,48},{88,56},{96,... | collective-permute-start | bytes 393224 | tf_op jit(solution)/shard_map/ppermute | solution.py:291
  28.9 1.6 %collective-permute-start.6 = (bf16[8,128,128]{2,1,0:T(8,128)(2,1)S(1)}, bf16[8,128,128]{2,1,0:T(8,128)(2,1)S(1)}, u32[]{:S(2)}, u32[]{:S(2)}) collective-permute-start(bf16[8,128,128]{2,1,0:T(8,128)(2,1)S(1)} %opposite_columns.1.refs_6_), channel_id=1, source_target_pairs={{0,8},{8,0},{16,24},{24,16},{32,40},{40,32},{48,56},{56,48},{64,72... | collective-permute-start | bytes 786440 | tf_op jit(solution)/shard_map/ppermute | solution.py:296
  33.6 9.6 %collective-permute-start.7 = (bf16[8,128,128]{2,1,0:T(8,128)(2,1)S(1)}, bf16[8,128,128]{2,1,0:T(8,128)(2,1)S(1)}, u32[]{:S(2)}, u32[]{:S(2)}) collective-permute-start(bf16[8,128,128]{2,1,0:T(8,128)(2,1)S(1)} %get-tuple-element.23), channel_id=1, source_target_pairs={{0,1},{1,2},{2,3},{3,0},{4,5},{5,6},{6,7},{7,4},{8,9},{9,10},{10,1... | collective-permute-start | bytes 786440 | tf_op jit(solution)/shard_map/ppermute | solution.py:291
  37.3 9.4 %copy-start.1 = (bf16[512,128]{1,0:T(8,128)(2,1)S(1)}, bf16[512,128]{1,0:T(8,128)(2,1)}, u32[]{:S(2)}) copy-start(bf16[512,128]{1,0:T(8,128)(2,1)} %refs_3_.1) | copy-start | bytes 393220
  37.3 8.0 %collective-permute-start.8 = (bf16[8,128,128]{2,1,0:T(8,128)(2,1)S(1)}, bf16[8,128,128]{2,1,0:T(8,128)(2,1)S(1)}, u32[]{:S(2)}, u32[]{:S(2)}) collective-permute-start(bf16[8,128,128]{2,1,0:T(8,128)(2,1)S(1)} %get-tuple-element.24), channel_id=1, source_target_pairs={{1,0},{2,1},{3,2},{0,3},{5,4},{6,5},{7,6},{4,7},{9,8},{10,9},{11,1... | collective-permute-start | bytes 786440 | tf_op jit(solution)/shard_map/ppermute | solution.py:291
  43.3 9.2 %collective-permute-start.9 = (bf16[4,128,128]{2,1,0:T(8,128)(2,1)S(1)}, bf16[4,128,128]{2,1,0:T(8,128)(2,1)S(1)}, u32[]{:S(2)}, u32[]{:S(2)}) collective-permute-start(bf16[4,128,128]{2,1,0:T(8,128)(2,1)S(1)} %add_convert_fusion.3), channel_id=1, source_target_pairs={{0,1},{1,2},{2,3},{3,0},{4,5},{5,6},{6,7},{7,4},{8,9},{9,10},{10,1... | collective-permute-start | bytes 393224 | tf_op jit(solution)/shard_map/ppermute | solution.py:291
  45.4 7.2 %collective-permute-start.10 = (bf16[4,128,128]{2,1,0:T(8,128)(2,1)S(1)}, bf16[4,128,128]{2,1,0:T(8,128)(2,1)S(1)}, u32[]{:S(2)}, u32[]{:S(2)}) collective-permute-start(bf16[4,128,128]{2,1,0:T(8,128)(2,1)S(1)} %add_convert_fusion.2), channel_id=1, source_target_pairs={{1,0},{2,1},{3,2},{0,3},{5,4},{6,5},{7,6},{4,7},{9,8},{10,9},{11,1... | collective-permute-start | bytes 393224 | tf_op jit(solution)/shard_map/ppermute | solution.py:291
  46.7 9.4 %collective-permute-start.12 = (bf16[512,128]{1,0:T(8,128)(2,1)S(1)}, bf16[512,128]{1,0:T(8,128)(2,1)S(1)}, u32[]{:S(2)}, u32[]{:S(2)}) collective-permute-start(bf16[512,128]{1,0:T(8,128)(2,1)S(1)} %copy-done.1), channel_id=1, source_target_pairs={{0,4},{1,5},{2,6},{3,7},{4,0},{5,1},{6,2},{7,3},{8,12},{9,13},{10,... | collective-permute-start | bytes 393224 | tf_op jit(solution)/shard_map/ppermute | solution.py:296
  52.5 8.4 %copy-start.2 = (bf16[128,128]{1,0:T(8,128)(2,1)S(1)}, bf16[128,128]{1,0:T(8,128)(2,1)}, u32[]{:S(2)}) copy-start(bf16[128,128]{1,0:T(8,128)(2,1)} %refs_2_.1) | copy-start | bytes 98308
  52.6 8.3 %collective-permute-start.11 = (bf16[8,128,128]{2,1,0:T(8,128)(2,1)S(1)}, bf16[8,128,128]{2,1,0:T(8,128)(2,1)S(1)}, u32[]{:S(2)}, u32[]{:S(2)}) collective-permute-start(bf16[8,128,128]{2,1,0:T(8,128)(2,1)S(1)} %row_sums.1.refs_0_), channel_id=1, source_target_pairs={{0,4},{1,5},{2,6},{3,7},{4,0},{5,1},{6,2},{7,3},{8,12},{9,13},{10,... | collective-permute-start | bytes 786440 | tf_op jit(solution)/shard_map/ppermute | solution.py:296
  62.2 10.6 %collective-permute-start.13 = (bf16[9,128,128]{2,1,0:T(8,128)(2,1)S(1)}, bf16[9,128,128]{2,1,0:T(8,128)(2,1)S(1)}, u32[]{:S(2)}, u32[]{:S(2)}) collective-permute-start(bf16[9,128,128]{2,1,0:T(8,128)(2,1)S(1)} %get-tuple-element.28.refs_5_.refs_8_), channel_id=1, source_target_pairs={{1,0},{2,1},{3,2},{0,3},{5,4},{6,5},{7,6},{4,7},{9,8},{10,9},{11,1... | collective-permute-start | bytes 884744 | tf_op jit(solution)/shard_map/ppermute | solution.py:291
  64.4 8.4 %collective-permute-start.14 = (bf16[9,128,128]{2,1,0:T(8,128)(2,1)S(1)}, bf16[9,128,128]{2,1,0:T(8,128)(2,1)S(1)}, u32[]{:S(2)}, u32[]{:S(2)}) collective-permute-start(bf16[9,128,128]{2,1,0:T(8,128)(2,1)S(1)} %get-tuple-element.28.refs_5_.refs_8_), channel_id=1, source_target_pairs={{0,1},{1,2},{2,3},{3,0},{4,5},{5,6},{6,7},{7,4},{8,9},{9,10},{10,1... | collective-permute-start | bytes 884744 | tf_op jit(solution)/shard_map/ppermute | solution.py:291
  72.8 6.4 %collective-permute-start.15 = (bf16[4,128,128]{2,1,0:T(8,128)(2,1)S(1)}, bf16[4,128,128]{2,1,0:T(8,128)(2,1)S(1)}, u32[]{:S(2)}, u32[]{:S(2)}) collective-permute-start(bf16[4,128,128]{2,1,0:T(8,128)(2,1)S(1)} %slice.36), channel_id=1, source_target_pairs={{0,1},{1,2},{2,3},{3,0},{4,5},{5,6},{6,7},{7,4},{8,9},{9,10},{10,1... | collective-permute-start | bytes 393224 | tf_op jit(solution)/shard_map/ppermute | solution.py:291
  72.9 6.3 %collective-permute-start.16 = (bf16[5,128,128]{2,1,0:T(8,128)(2,1)S(1)}, bf16[5,128,128]{2,1,0:T(8,128)(2,1)S(1)}, u32[]{:S(2)}, u32[]{:S(2)}) collective-permute-start(bf16[5,128,128]{2,1,0:T(8,128)(2,1)S(1)} %slice.37), channel_id=1, source_target_pairs={{1,0},{2,1},{3,2},{0,3},{5,4},{6,5},{7,6},{4,7},{9,8},{10,9},{11,1... | collective-permute-start | bytes 491528 | tf_op jit(solution)/shard_map/ppermute | solution.py:291
  81.3 2.8 %collective-permute-start.17 = (bf16[33,128,128]{2,1,0:T(8,128)(2,1)S(1)}, bf16[33,128,128]{2,1,0:T(8,128)(2,1)S(1)}, u32[]{:S(2)}, u32[]{:S(2)}) collective-permute-start(bf16[33,128,128]{2,1,0:T(8,128)(2,1)S(1)} %get-tuple-element.29), channel_id=1, source_target_pairs={{0,8},{8,0},{16,24},{24,16},{32,40},{40,32},{48,56},{56,48},{64,72... | collective-permute-start | bytes 3244040 | tf_op jit(solution)/shard_map/ppermute | solution.py:296
  84.3 12.9 %collective-permute-start.18 = (bf16[9,128,128]{2,1,0:T(8,128)(2,1)S(1)}, bf16[9,128,128]{2,1,0:T(8,128)(2,1)S(1)}, u32[]{:S(2)}, u32[]{:S(2)}) collective-permute-start(bf16[9,128,128]{2,1,0:T(8,128)(2,1)S(1)} %get-tuple-element.32.refs_5_), channel_id=1, source_target_pairs={{0,32},{8,40},{16,48},{24,56},{32,64},{40,72},{48,80},{56,88},{64,... | collective-permute-start | bytes 884744 | tf_op jit(solution)/shard_map/ppermute | solution.py:291
  89.3 7.9 %collective-permute-start.19 = (bf16[9,128,128]{2,1,0:T(8,128)(2,1)S(1)}, bf16[9,128,128]{2,1,0:T(8,128)(2,1)S(1)}, u32[]{:S(2)}, u32[]{:S(2)}) collective-permute-start(bf16[9,128,128]{2,1,0:T(8,128)(2,1)S(1)} %get-tuple-element.33), channel_id=1, source_target_pairs={{32,0},{40,8},{48,16},{56,24},{64,32},{72,40},{80,48},{88,56},{96,... | collective-permute-start | bytes 884744 | tf_op jit(solution)/shard_map/ppermute | solution.py:291
  97.2 7.3 %collective-permute-start.20 = (bf16[5,128,128]{2,1,0:T(8,128)(2,1)S(1)}, bf16[5,128,128]{2,1,0:T(8,128)(2,1)S(1)}, u32[]{:S(2)}, u32[]{:S(2)}) collective-permute-start(bf16[5,128,128]{2,1,0:T(8,128)(2,1)S(1)} %add_convert_fusion), channel_id=1, source_target_pairs={{0,32},{8,40},{16,48},{24,56},{32,64},{40,72},{48,80},{56,88},{64,... | collective-permute-start | bytes 491528 | tf_op jit(solution)/shard_map/ppermute | solution.py:291
  97.3 5.8 %collective-permute-start.21 = (bf16[4,128,128]{2,1,0:T(8,128)(2,1)S(1)}, bf16[4,128,128]{2,1,0:T(8,128)(2,1)S(1)}, u32[]{:S(2)}, u32[]{:S(2)}) collective-permute-start(bf16[4,128,128]{2,1,0:T(8,128)(2,1)S(1)} %add_convert_fusion.1), channel_id=1, source_target_pairs={{32,0},{40,8},{48,16},{56,24},{64,32},{72,40},{80,48},{88,56},{96,... | collective-permute-start | bytes 393224 | tf_op jit(solution)/shard_map/ppermute | solution.py:291
  104.5 5.4 %collective-permute-start.22 = (bf16[5,128,128]{2,1,0:T(8,128)(2,1)S(1)}, bf16[5,128,128]{2,1,0:T(8,128)(2,1)S(1)}, u32[]{:S(2)}, u32[]{:S(2)}) collective-permute-start(bf16[5,128,128]{2,1,0:T(8,128)(2,1)S(1)} %far_columns.1.refs_5_), channel_id=1, source_target_pairs={{0,16},{8,24},{16,0},{24,8},{32,48},{40,56},{48,32},{56,40},{64,80... | collective-permute-start | bytes 491528 | tf_op jit(solution)/shard_map/ppermute | solution.py:296

commit v2 on v1

--- a/solution.py
+++ b/solution.py
@@ -163,6 +163,21 @@
         at += size
 
 
+def finish_parts(first, acc, extra_refs, out_refs):
+    early = extra_refs[0]
+    at = 0
+    for ref in out_refs:
+        size = ref.shape[0]
+        total = acc[at : at + size] + early[first + at : first + at + size]
+        ref[...] = total.astype(ref.dtype)
+        at += size
+
+
+def finish_near(acc, extra_refs, out_refs):
+    out_refs[0][...] = acc[...]
+    out_refs[1][...] = extra_refs[0][...]
+
+
 def finish_early(acc, extra_refs, out_refs):
     del extra_refs
     out_refs[0][...] = acc[...]
@@ -217,7 +232,11 @@
     return jnp.concatenate([first, second], 0)
 
 
-def sums_kernel(keep_far, keep, plus, minus, plus2, minus2, out_ref):
+def sums_kernel(
+    keep_far, keep, plus, minus, plus2, minus2, rows, cols, out_ref, rows_out, cols_out
+):
+    rows_out[...] = rows[...]
+    cols_out[...] = cols[...]
     out_ref[0:4] = own_sum(keep, plus, minus, plus2, minus2, False, 0).astype(BF16)
     out_ref[4:8] = own_sum(keep_far, plus, minus, plus2, minus2, True, 0).astype(BF16)
 
@@ -236,7 +255,7 @@
         value, slope = gelu_pair(pre_act)
         if at == 0:
             out_ref[...] = value.astype(BF16)
-        grad_pre = (block_cotangent[...].astype(F32) * slope).astype(BF16)
+        grad_pre = (block_cotangent[...].reshape(4 * TS, TS).astype(F32) * slope).astype(BF16)
         for i in range(4):
             pair_ref[at + i] = lax.dot_general(
                 w,
@@ -252,6 +271,30 @@
     pair_ref[8] = (terms[0] + terms[1]).astype(BF16)
 
 
+def near_kernel(own, following, previous, near_out, first_out, second_out):
+    near_out[0:8] = own[...]
+    near_out[8:16] = following[...]
+    near_out[16:24] = previous[...]
+    first_out[...] = previous[0:4]
+    second_out[...] = following[4:8]
+
+
+def columns_kernel(near, first, second, cotangent, out_ref, cotangent_out):
+    out_ref[0:24] = near[...]
+    out_ref[24:28] = first[...]
+    out_ref[28:32] = second[...]
+    cotangent_out[...] = cotangent[...]
+
+
+def join(name, *parts):
+    return pl.pallas_call(
+        join_kernel,
+        out_shape=array(sum(p.shape[0] for p in parts)),
+        compiler_params=pltpu.CompilerParams(vmem_limit_bytes=VMEM_LIMIT),
+        name=name,
+    )(*parts)
+
+
 def join_kernel(*refs):
     at = 0
     for ref in refs[:-1]:
@@ -304,57 +347,69 @@
 
     owner = rows >> 2
     row_at = (((owner ^ gc) >> 2) & 1) * 16 + ((owner - gc) & 3) * 4 + (rows & 3)
-    row_sent, row_arrived = look_up(row_at, sent), look_up(row_at, arrived)
+    row_sent = look_up(row_at, sent)
     holder = cols >> 2
     core = (holder ^ gr) & 1
     col_at = (((holder ^ gr) >> 1) & 1) * 16 + (((holder >> 2) - (gr >> 2)) & 3) * 4 + (cols & 3)
-    col_sent, col_arrived = look_up(col_at, sent), look_up(col_at, arrived)
-    forward_plan = group_plan(row_sent, core * 32 + col_arrived, live, (0, 16, 32), 4, 16, 64)
-    theirs_key = jnp.where(row_arrived < 24, 0, 32) + col_sent
-    back_key = jnp.where(core == 1, theirs_key, 64 + col_sent)
-    backward_plan = group_plan(back_key, row_arrived, live, (0, 32, 64, 80, 96), 2, 16, 32)
-
+    col_arrived = look_up(col_at, arrived)
+    near_own = (core == 0) & (col_arrived < 24)
+    forward_key = jnp.where(near_own, 0, 32) + row_sent
+    forward_plan = group_plan(
+        forward_key, core * 32 + col_arrived, live, (0, 32, 48, 64), 2, 32, 64
+    )
     core_swap, y_swap = pair_permute("gr", 1), pair_permute("gr", 2)
     w_swap = pair_permute("gc", 4)
     z_up, z_down = ring_permutes("gr")
     x_up, x_down = ring_permutes("gc")
 
     own = features.reshape(4, TS, TS)
-    far = y_swap(own)
-    pair = jnp.concatenate([own, far], 0)
+    pair = jnp.concatenate([own, y_swap(own)], 0)
     previous, following = z_up(pair), z_down(pair)
     blocks = pltpu.with_memory_space_constraint(tiles[0, 0], pltpu.VMEM)
     held = call(join_kernel, array(8), "after_tiles", blocks, pair)
-    near = call(join_kernel, array(24), "near_columns", blocks, held, following, previous)
-    opposite = call(
-        join_kernel, array(8), "opposite_columns",
-        blocks, z_up(previous[:4]), z_down(following[4:8]),
-    )
-    tables = [
-        (near, 0, 0, 24),
-        (opposite, 24, 0, 8),
-        (core_swap(near), 32, 0, 24),
-        (core_swap(opposite), 56, 0, 8),
-    ]
+    near, first, second = call(
+        near_kernel, [array(24), array(4), array(4)], "near_columns",
+        blocks, held, following, previous,
+    )
+    opposite_near, opposite_far = z_up(first), z_down(second)
+    early, near = group_pass(
+        forward_plan, blocks, [(near, 0, 0, 24)], 64, 0, (0, 32), 2, 32, True, [near],
+        [array(32, F32), array(24)], finish_near, "forward_early",
+    )
+    columns, own_cotangent = call(
+        columns_kernel, [array(32), array(4)], "own_columns",
+        blocks, near, opposite_near, opposite_far, cotangent.reshape(4, TS, TS),
+    )
+    tables = [(columns, 0, 0, 32), (core_swap(columns), 32, 0, 32)]
+    far_cotangent = w_swap(own_cotangent)
     plus, minus = group_pass(
-        forward_plan, blocks, tables, 64, 0, (0, 16), 4, 16, True, [], [array(8)] * 2, write_parts,
-        "forward_sent",
+        forward_plan, blocks, tables, 64, 1, (32, 48), 2, 32, True, [early],
+        [array(8)] * 2, functools.partial(finish_parts, 0), "forward_sent",
     )
 
     got_plus, got_minus = x_up(plus), x_down(minus)
     plus2, minus2, keep_far, keep = group_pass(
-        forward_plan, blocks, tables, 64, 1, (16, 32), 4, 16, True, [],
-        [array(4), array(4), array(4, F32), array(4, F32)], write_parts, "forward_kept",
+        forward_plan, blocks, tables, 64, 2, (48, 64), 2, 32, True, [early, far_cotangent],
+        [array(4), array(4), array(4, F32), array(4, F32)], functools.partial(finish_parts, 16),
+        "forward_kept",
     )
     got_plus2 = x_up((plus2.astype(F32) + got_plus[:4].astype(F32)).astype(BF16))
     got_minus2 = x_down((minus2.astype(F32) + got_minus[:4].astype(F32)).astype(BF16))
     got = (got_plus, got_minus, got_plus2, got_minus2)
-    sums = call(sums_kernel, array(8), "row_sums", blocks, keep_far, keep, *got)
+    sums, later_rows, later_cols = call(
+        sums_kernel, [array(8), row_at, col_at], "row_sums",
+        blocks, keep_far, keep, *got, row_at, col_at,
+    )
+    row_arrived, col_sent = look_up(later_rows, arrived), look_up(later_cols, sent)
+    theirs_key = jnp.where(row_arrived < 24, 0, 32) + col_sent
+    back_key = jnp.where(core == 1, theirs_key, 64 + col_sent)
+    backward_plan = group_plan(back_key, row_arrived, live, (0, 32, 64, 80, 96), 2, 32, 32)
+
     output, pair = call(
         middle_kernel,
         [jax.ShapeDtypeStruct(cotangent.shape, BF16), array(9)],
         "middle",
-        blocks, sums, w_swap(sums), weight, cotangent, w_swap(cotangent),
+        blocks, sums, w_swap(sums), weight, cotangent, far_cotangent,
     )
 
     previous, following = x_up(pair), x_down(pair)
@@ -362,24 +417,24 @@
     early = [(pair, 0, 0, 8), (following, 8, 0, 8), (previous, 16, 0, 8)]
     late = [(opposite_near, 24, 0, 4), (opposite_far, 28, 0, 4)]
     (sums,) = group_pass(
-        backward_plan, blocks, early, 32, 0, (0, 32), 2, 16, False, [], [array(32, F32)],
+        backward_plan, blocks, early, 32, 0, (0, 32), 2, 32, False, [], [array(32, F32)],
         finish_early, "backward_early",
     )
     theirs, weight_part = group_pass(
-        backward_plan, blocks, late, 32, 1, (32, 64), 2, 16, False,
+        backward_plan, blocks, late, 32, 1, (32, 64), 2, 32, False,
         [sums, pair, following, previous, opposite_far], [array(33), array(1)],
         finish_theirs, "backward_theirs",
     )
 
     got = core_swap(theirs)
     (mine,) = group_pass(
-        backward_plan, blocks, early + late, 32, 2, (64, 80), 2, 16, False, [], [array(16)],
+        backward_plan, blocks, early + late, 32, 2, (64, 80), 2, 32, False, [], [array(16)],
         write_parts, "backward_sent",
     )
     plus, minus = call(add_core_kernel, [array(9)] * 2, "add_core", blocks, mine, got, weight_part)
     got_plus, got_minus = z_up(plus), z_down(minus)
     plus2, minus2, keep_far, keep = group_pass(
-        backward_plan, blocks, early + late, 32, 3, (80, 96), 2, 16, False, [got],
+        backward_plan, blocks, early + late, 32, 3, (80, 96), 2, 32, False, [got],
         [array(5), array(4), array(4, F32), array(4, F32)], finish_mine, "backward_kept",
     )
     got_plus2 = z_up((plus2.astype(F32) + got_plus[:5].astype(F32)).astype(BF16))

time: 113 us -> 111 us (0.982); the launches traced: 111 us -> 111 us
  Pallas kernels: 17.5 us -> 29.9 us
  starting transfers between devices: 39.4 us -> 29.9 us
  waiting for transfers between devices: 37.3 us -> 35.3 us
    pallas_call x6 -> x7, Pallas kernels: 15.1 us -> 27.4 us  [group_pass(): pl.pallas_call(functools.partial(group_kernel, tuple((t[1:] for t in tabl...]
    ppermute x8, waiting for transfers between devices: 2.59 us -> 12.8 us  [ring_permutes(): lax.ppermute(v, axis, down)]
    ppermute x8, waiting for transfers between devices: 22.3 us -> 12.7 us  [ring_permutes(): lax.ppermute(v, axis, up)]
    ppermute x8, starting transfers between devices: 11 us -> 5.44 us  [ring_permutes(): lax.ppermute(v, axis, up)]
    ppermute x7 -> x6, starting transfers between devices: 10.6 us -> 7.9 us  [pair_permute(): lax.ppermute(value, axis, [(i, i ^ mask) for i in range(size)])]
    ppermute x7 -> x6, waiting for transfers between devices: 12.4 us -> 9.8 us  [pair_permute(): lax.ppermute(value, axis, [(i, i ^ mask) for i in range(size)])]
    select_n x2 -> x0, other arithmetic: 1.47 us -> none  [look_up(): total = jnp.where(index == at, value, total)]
    ppermute x8, starting transfers between devices: 17.8 us -> 16.5 us  [ring_permutes(): lax.ppermute(v, axis, down)]
  transfers between devices with their start and end apart: 23 -> 22, of which waited for: 12 -> 10; matrix products, arithmetic and copies ran while one was open for 5% -> 4% of each run, Pallas kernels for 9% -> 22%
where the time goes in v2:
time: 111 us
  waiting for transfers between devices  35.3 us (32%)
  starting transfers between devices  29.9 us (27%)
  Pallas kernels  29.9 us (27%)
  local copies, waits for them, and re-layouts  7.91 us (7%)
  other arithmetic  5.86 us (5%)
  between operations  1.7 us (2%)
    pallas_call x7, Pallas kernels, group_pass(): pl.pallas_call(functools.partial(group_kernel, tuple((t[1:] for t in tabl...  27.4 us
    ppermute x8, starting transfers between devices, ring_permutes(): lax.ppermute(v, axis, down)  16.5 us
    ppermute x8, waiting for transfers between devices, ring_permutes(): lax.ppermute(v, axis, down)  12.8 us
    ppermute x8, waiting for transfers between devices, ring_permutes(): lax.ppermute(v, axis, up)  12.7 us
    ppermute x6, waiting for transfers between devices, pair_permute(): lax.ppermute(value, axis, [(i, i ^ mask) for i in range(size)])  9.8 us
    ppermute x6, starting transfers between devices, pair_permute(): lax.ppermute(value, axis, [(i, i ^ mask) for i in range(size)])  7.9 us
    unnamed x18, local copies, waits for them, and re-layouts  7.89 us
    ppermute x8, starting transfers between devices, ring_permutes(): lax.ppermute(v, axis, up)  5.44 us
  transfers between devices with their start and end apart: 22, of which 10 were waited for; matrix products, arithmetic and copies ran while one was open for 4% of the time, Pallas kernels for 22%

profile of v2, /device:TPU:0, one launch (start us, length us, event | category | flops | bytes accessed | tf_op | source)
XLA Modules:
  0.0 110.5 jit_solution(4135226310082800493)
XLA Ops:
  0.6 1.7 %collective-permute-start = (bf16[4,128,128]{2,1,0:T(8,128)(2,1)}, bf16[4,128,128]{2,1,0:T(8,128)(2,1)S(1)}, u32[]{:S(2)}, u32[]{:S(2)}) collective-permute-start(bf16[4,128,128]{2,1,0:T(8,128)(2,1)} %bitcast.26), channel_id=1, source_target_pairs={{0,16},{8,24},{16,0},{24,8},{32,48},{40,56},{48,32},{56,40},{64,80... | collective-permute-start | bytes 393224 | tf_op jit(solution)/shard_map/ppermute | solution.py:339
  2.4 0.7 multiply_reduce_fusion
  3.8 0.7 add_reduce_fusion.refs_6_
  4.5 0.1 convert_reduce_fusion.4
  4.7 0.1 select_reduce_fusion.11
  4.8 0.2 select_reduce_fusion.5
  5.0 0.4 convert_reduce_fusion.1
  5.7 0.4 select_reduce_fusion.1
  6.1 0.9 pad_maximum_fusion.refs_0_
  7.0 4.3 %collective-permute-start.1 = (bf16[8,128,128]{2,1,0:T(8,128)(2,1)S(1)}, bf16[8,128,128]{2,1,0:T(8,128)(2,1)S(1)}, u32[]{:S(2)}, u32[]{:S(2)}) collective-permute-start(bf16[8,128,128]{2,1,0:T(8,128)(2,1)S(1)} %pad_maximum_fusion.refs_0_), channel_id=1, source_target_pairs={{32,0},{40,8},{48,16},{56,24},{64,32},{72,40},{80,48},{88,56},{96,... | collective-permute-start | bytes 786440 | tf_op jit(solution)/shard_map/ppermute | solution.py:334
  11.4 7.8 %copy-done = bf16[1,1,736,128,128]{4,3,2,1,0:T(8,128)(2,1)S(1)} copy-done((bf16[1,1,736,128,128]{4,3,2,1,0:T(8,128)(2,1)S(1)}, bf16[1,1,736,128,128]{4,3,2,1,0:T(8,128)(2,1)}, u32[]{:S(2)}) %copy-start) | copy-done | bytes 24117272
  19.3 0.5 collective-permute-done.2.refs_2_
  20.0 3.2 %collective-permute-start.4 = (bf16[4,128,128]{2,1,0:T(8,128)(2,1)S(1)}, bf16[4,128,128]{2,1,0:T(8,128)(2,1)S(1)}, u32[]{:S(2)}, u32[]{:S(2)}) collective-permute-start(bf16[4,128,128]{2,1,0:T(8,128)(2,1)S(1)} %get-tuple-element.34), channel_id=1, source_target_pairs={{32,0},{40,8},{48,16},{56,24},{64,32},{72,40},{80,48},{88,56},{96,... | collective-permute-start | bytes 393224 | tf_op jit(solution)/shard_map/ppermute | solution.py:334
  23.2 4.8 %forward_early.1 = (f32[32,128,128]{2,1,0:T(8,128)S(1)}, bf16[24,128,128]{2,1,0:T(8,128)(2,1)S(1)}) custom-call(s32[4]{0:T(128)S(1)} %select_reduce_fusion.10.refs_0_, s32[1024]{0:T(1024)S(1)} %get-tuple-element.70.refs_1_, s32[1024]{0:T(1024)S(1)} %get-tuple-element.69.refs_2_, s32[512]{0:T(512)S(1)} %broadcast_add_fusion.1.refs_3_, ...), custom_call_target="tpu_custom_call" | custom-call | flops 12348030976 | bytes 4194304 | tf_op jit(solution)/shard_map/forward_early/pallas_call | solution.py:125
  28.2 3.0 %collective-permute-start.6 = (bf16[4,128,128]{2,1,0:T(8,128)(2,1)S(1)}, bf16[4,128,128]{2,1,0:T(8,128)(2,1)S(1)}, u32[]{:S(2)}, u32[]{:S(2)}) collective-permute-start(bf16[4,128,128]{2,1,0:T(8,128)(2,1)S(1)} %get-tuple-element.37), channel_id=1, source_target_pairs={{0,4},{1,5},{2,6},{3,7},{4,0},{5,1},{6,2},{7,3},{8,12},{9,13},{10,... | collective-permute-start | bytes 393224 | tf_op jit(solution)/shard_map/ppermute | solution.py:339
  31.2 4.0 %forward_sent.1 = (bf16[8,128,128]{2,1,0:T(8,128)(2,1)S(1)}, bf16[8,128,128]{2,1,0:T(8,128)(2,1)S(1)}) custom-call(s32[4]{0:T(128)S(1)} %select_reduce_fusion.10.refs_0_, s32[1024]{0:T(1024)S(1)} %get-tuple-element.70.refs_1_, s32[1024]{0:T(1024)S(1)} %get-tuple-element.69.refs_2_, s32[512]{0:T(512)S(1)} %broadcast_add_fusion.1.refs_3_, ...), custom_call_target="tpu_custom_call" | custom-call | flops 6174015488 | bytes 4194304 | tf_op jit(solution)/shard_map/forward_sent/pallas_call | solution.py:125
  35.2 0.2 collective-permute-start.8
  35.5 1.9 %collective-permute-start.7 = (bf16[8,128,128]{2,1,0:T(8,128)(2,1)S(1)}, bf16[8,128,128]{2,1,0:T(8,128)(2,1)S(1)}, u32[]{:S(2)}, u32[]{:S(2)}) collective-permute-start(bf16[8,128,128]{2,1,0:T(8,128)(2,1)S(1)} %get-tuple-element.40), channel_id=1, source_target_pairs={{0,1},{1,2},{2,3},{3,0},{4,5},{5,6},{6,7},{7,4},{8,9},{9,10},{10,1... | collective-permute-start | bytes 786440 | tf_op jit(solution)/shard_map/ppermute | solution.py:334
  37.3 4.0 %forward_kept.1 = (bf16[4,128,128]{2,1,0:T(8,128)(2,1)S(1)}, bf16[4,128,128]{2,1,0:T(8,128)(2,1)S(1)}, f32[4,128,128]{2,1,0:T(8,128)S(1)}, f32[4,128,128]{2,1,0:T(8,128)S(1)}) custom-call(s32[4]{0:T(128)S(1)} %select_reduce_fusion.10.refs_0_, s32[1024]{0:T(1024)S(1)} %get-tuple-element.70.refs_1_, s32[1024]{0:T(1024)S(1)} %get-tuple-element.69.refs_2_, ...), custom_call_target="tpu_custom_call" | custom-call | flops 6174015488 | bytes 4194304 | tf_op jit(solution)/shard_map/forward_kept/pallas_call | solution.py:125
  41.3 0.8 collective-permute-done.8.refs_3_
  42.2 2.2 %collective-permute-start.10 = (bf16[4,128,128]{2,1,0:T(8,128)(2,1)S(1)}, bf16[4,128,128]{2,1,0:T(8,128)(2,1)S(1)}, u32[]{:S(2)}, u32[]{:S(2)}) collective-permute-start(bf16[4,128,128]{2,1,0:T(8,128)(2,1)S(1)} %add_convert_fusion.2), channel_id=1, source_target_pairs={{1,0},{2,1},{3,2},{0,3},{5,4},{6,5},{7,6},{4,7},{9,8},{10,9},{11,1... | collective-permute-start | bytes 393224 | tf_op jit(solution)/shard_map/ppermute | solution.py:334
  44.5 2.7 %collective-permute-done.10.refs_5_ = bf16[4,128,128]{2,1,0:T(8,128)(2,1)S(1)} collective-permute-done((bf16[4,128,128]{2,1,0:T(8,128)(2,1)S(1)}, bf16[4,128,128]{2,1,0:T(8,128)(2,1)S(1)}, u32[]{:S(2)}, u32[]{:S(2)}) %collective-permute-start.10) | collective-permute-done | bytes 131104 | tf_op jit(solution)/shard_map/ppermute | solution.py:334
  47.2 3.4 %collective-permute-done.9.refs_4_ = bf16[4,128,128]{2,1,0:T(8,128)(2,1)S(1)} collective-permute-done((bf16[4,128,128]{2,1,0:T(8,128)(2,1)S(1)}, bf16[4,128,128]{2,1,0:T(8,128)(2,1)S(1)}, u32[]{:S(2)}, u32[]{:S(2)}) %collective-permute-start.9) | collective-permute-done | bytes 131104 | tf_op jit(solution)/shard_map/ppermute | solution.py:334
  50.9 0.1 convert_reduce_fusion.2
  51.1 0.2 select_reduce_fusion.4
  51.3 0.4 convert_reduce_fusion
  51.7 2.8 %collective-permute-start.11 = (bf16[8,128,128]{2,1,0:T(8,128)(2,1)S(1)}, bf16[8,128,128]{2,1,0:T(8,128)(2,1)S(1)}, u32[]{:S(2)}, u32[]{:S(2)}) collective-permute-start(bf16[8,128,128]{2,1,0:T(8,128)(2,1)S(1)} %get-tuple-element.44.refs_0_), channel_id=1, source_target_pairs={{0,4},{1,5},{2,6},{3,7},{4,0},{5,1},{6,2},{7,3},{8,12},{9,13},{10,... | collective-permute-start | bytes 786440 | tf_op jit(solution)/shard_map/ppermute | solution.py:339
  54.7 0.5 select_reduce_fusion
  55.2 4.4 %collective-permute-done.11.refs_1_ = bf16[8,128,128]{2,1,0:T(8,128)(2,1)S(1)} collective-permute-done((bf16[8,128,128]{2,1,0:T(8,128)(2,1)S(1)}, bf16[8,128,128]{2,1,0:T(8,128)(2,1)S(1)}, u32[]{:S(2)}, u32[]{:S(2)}) %collective-permute-start.11) | collective-permute-done | bytes 262176 | tf_op jit(solution)/shard_map/ppermute | solution.py:339
  59.6 1.3 %middle.1 = (bf16[512,128]{1,0:T(8,128)(2,1)}, bf16[9,128,128]{2,1,0:T(8,128)(2,1)S(1)}) custom-call(bf16[736,128,128]{2,1,0:T(8,128)(2,1)S(1)} %bitcast.17, bf16[8,128,128]{2,1,0:T(8,128)(2,1)S(1)} %get-tuple-element.44.refs_0_, bf16[8,128,128]{2,1,0:T(8,128)(2,1)S(1)} %collective-permute-done.11.refs_1_, bf16[128,128]{1,0:T(8,128)(2,1)S(1)} %copy-done.2, ...), custom_call_target="tpu_custom_call" | custom-call | tf_op jit(solution)/shard_map/middle/pallas_call | solution.py:208
  60.9 0.6 collective-permute-start.12
  61.5 1.4 %collective-permute-start.13 = (bf16[9,128,128]{2,1,0:T(8,128)(2,1)S(1)}, bf16[9,128,128]{2,1,0:T(8,128)(2,1)S(1)}, u32[]{:S(2)}, u32[]{:S(2)}) collective-permute-start(bf16[9,128,128]{2,1,0:T(8,128)(2,1)S(1)} %get-tuple-element.48.refs_5_.refs_8_), channel_id=1, source_target_pairs={{0,1},{1,2},{2,3},{3,0},{4,5},{5,6},{6,7},{7,4},{8,9},{9,10},{10,1... | collective-permute-start | bytes 884744 | tf_op jit(solution)/shard_map/ppermute | solution.py:334
  63.0 6.4 %collective-permute-done.12.refs_6_.refs_9_ = bf16[9,128,128]{2,1,0:T(8,128)(2,1)S(1)} collective-permute-done((bf16[9,128,128]{2,1,0:T(8,128)(2,1)S(1)}, bf16[9,128,128]{2,1,0:T(8,128)(2,1)S(1)}, u32[]{:S(2)}, u32[]{:S(2)}) %collective-permute-start.12) | collective-permute-done | bytes 294944 | tf_op jit(solution)/shard_map/ppermute | solution.py:334
  69.4 0.4 collective-permute-start.15
  69.8 1.9 %collective-permute-start.14 = (bf16[4,128,128]{2,1,0:T(8,128)(2,1)S(1)}, bf16[4,128,128]{2,1,0:T(8,128)(2,1)S(1)}, u32[]{:S(2)}, u32[]{:S(2)}) collective-permute-start(bf16[4,128,128]{2,1,0:T(8,128)(2,1)S(1)} %slice.26), channel_id=1, source_target_pairs={{0,1},{1,2},{2,3},{3,0},{4,5},{5,6},{6,7},{7,4},{8,9},{9,10},{10,1... | collective-permute-start | bytes 393224 | tf_op jit(solution)/shard_map/ppermute | solution.py:334
  71.8 4.8 %backward_early.1.refs_7_ = f32[32,128,128]{2,1,0:T(8,128)S(1)} custom-call(s32[5]{0:T(128)S(1)} %select_reduce_fusion.7.refs_0_, s32[1088]{0:T(1024)S(1)} %get-tuple-element.68.refs_1_, s32[1088]{0:T(1024)S(1)} %get-tuple-element.67.refs_2_, s32[544]{0:T(1024)S(1)} %broadcast_add_fusion.refs_3_, bf16[736,128,128]{2,1,0:T(8,128)(2,1)S(1)} %bitcast.18, ...), custom_call_target="tpu_custom_call" | custom-call | flops 8220835840 | bytes 4194304 | tf_op jit(solution)/shard_map/backward_early/pallas_call | solution.py:125
  76.6 2.6 %backward_theirs.1 = (bf16[33,128,128]{2,1,0:T(8,128)(2,1)S(1)}, bf16[1,128,128]{2,1,0:T(8,128)(2,1)S(1)}) custom-call(s32[5]{0:T(128)S(1)} %select_reduce_fusion.7.refs_0_, s32[1088]{0:T(1024)S(1)} %get-tuple-element.68.refs_1_, s32[1088]{0:T(1024)S(1)} %get-tuple-element.67.refs_2_, s32[544]{0:T(1024)S(1)} %broadcast_add_fusion.refs_3_, ...), custom_call_target="tpu_custom_call" | custom-call | flops 8220835840 | bytes 4194304 | tf_op jit(solution)/shard_map/backward_theirs/pallas_call | solution.py:125
  79.3 3.9 %backward_sent.1.refs_0_ = bf16[16,128,128]{2,1,0:T(8,128)(2,1)S(1)} custom-call(s32[5]{0:T(128)S(1)} %select_reduce_fusion.7.refs_0_, s32[1088]{0:T(1024)S(1)} %get-tuple-element.68.refs_1_, s32[1088]{0:T(1024)S(1)} %get-tuple-element.67.refs_2_, s32[544]{0:T(1024)S(1)} %broadcast_add_fusion.refs_3_, bf16[736,128,128]{2,1,0:T(8,128)(2,1)S(1)} %bitcast.20, ...), custom_call_target="tpu_custom_call" | custom-call | flops 4093640704 | bytes 4194304 | tf_op jit(solution)/shard_map/backward_sent/pallas_call | solution.py:125
  83.2 0.1 add_core.1
  83.4 2.3 %collective-permute-start.18 = (bf16[9,128,128]{2,1,0:T(8,128)(2,1)S(1)}, bf16[9,128,128]{2,1,0:T(8,128)(2,1)S(1)}, u32[]{:S(2)}, u32[]{:S(2)}) collective-permute-start(bf16[9,128,128]{2,1,0:T(8,128)(2,1)S(1)} %get-tuple-element.53), channel_id=1, source_target_pairs={{32,0},{40,8},{48,16},{56,24},{64,32},{72,40},{80,48},{88,56},{96,... | collective-permute-start | bytes 884744 | tf_op jit(solution)/shard_map/ppermute | solution.py:334
  85.7 3.2 %backward_kept.1 = (bf16[5,128,128]{2,1,0:T(8,128)(2,1)S(1)}, bf16[4,128,128]{2,1,0:T(8,128)(2,1)S(1)}, f32[4,128,128]{2,1,0:T(8,128)S(1)}, f32[4,128,128]{2,1,0:T(8,128)S(1)}) custom-call(s32[5]{0:T(128)S(1)} %select_reduce_fusion.7.refs_0_, s32[1088]{0:T(1024)S(1)} %get-tuple-element.68.refs_1_, s32[1088]{0:T(1024)S(1)} %get-tuple-element.67.refs_2_, ...), custom_call_target="tpu_custom_call" | custom-call | flops 4093640704 | bytes 4194304 | tf_op jit(solution)/shard_map/backward_kept/pallas_call | solution.py:125
  88.9 7.4 %collective-permute-done.17.refs_1_ = bf16[9,128,128]{2,1,0:T(8,128)(2,1)S(1)} collective-permute-done((bf16[9,128,128]{2,1,0:T(8,128)(2,1)S(1)}, bf16[9,128,128]{2,1,0:T(8,128)(2,1)S(1)}, u32[]{:S(2)}, u32[]{:S(2)}) %collective-permute-start.17) | collective-permute-done | bytes 294944 | tf_op jit(solution)/shard_map/ppermute | solution.py:334
  96.6 3.3 %collective-permute-start.20 = (bf16[4,128,128]{2,1,0:T(8,128)(2,1)S(1)}, bf16[4,128,128]{2,1,0:T(8,128)(2,1)S(1)}, u32[]{:S(2)}, u32[]{:S(2)}) collective-permute-start(bf16[4,128,128]{2,1,0:T(8,128)(2,1)S(1)} %add_convert_fusion.1), channel_id=1, source_target_pairs={{32,0},{40,8},{48,16},{56,24},{64,32},{72,40},{80,48},{88,56},{96,... | collective-permute-start | bytes 393224 | tf_op jit(solution)/shard_map/ppermute | solution.py:334
  99.8 2.9 %collective-permute-done.20.refs_4_ = bf16[4,128,128]{2,1,0:T(8,128)(2,1)S(1)} collective-permute-done((bf16[4,128,128]{2,1,0:T(8,128)(2,1)S(1)}, bf16[4,128,128]{2,1,0:T(8,128)(2,1)S(1)}, u32[]{:S(2)}, u32[]{:S(2)}) %collective-permute-start.20) | collective-permute-done | bytes 131104 | tf_op jit(solution)/shard_map/ppermute | solution.py:334
  102.7 1.3 %collective-permute-done.19.refs_3_ = bf16[5,128,128]{2,1,0:T(8,128)(2,1)S(1)} collective-permute-done((bf16[5,128,128]{2,1,0:T(8,128)(2,1)S(1)}, bf16[5,128,128]{2,1,0:T(8,128)(2,1)S(1)}, u32[]{:S(2)}, u32[]{:S(2)}) %collective-permute-start.19) | collective-permute-done | bytes 163872 | tf_op jit(solution)/shard_map/ppermute | solution.py:334
  104.1 0.3 collective-permute-start.21
  104.4 5.4 %collective-permute-done.21.refs_6_ = bf16[5,128,128]{2,1,0:T(8,128)(2,1)S(1)} collective-permute-done((bf16[5,128,128]{2,1,0:T(8,128)(2,1)S(1)}, bf16[5,128,128]{2,1,0:T(8,128)(2,1)S(1)}, u32[]{:S(2)}, u32[]{:S(2)}) %collective-permute-start.21) | collective-permute-done | bytes 163872 | tf_op jit(solution)/shard_map/ppermute | solution.py:339
  109.7 0.8 last.1
  (75 shorter events, 2.1 us)
Async XLA Ops:
  0.6 5.4 %collective-permute-start = (bf16[4,128,128]{2,1,0:T(8,128)(2,1)}, bf16[4,128,128]{2,1,0:T(8,128)(2,1)S(1)}, u32[]{:S(2)}, u32[]{:S(2)}) collective-permute-start(bf16[4,128,128]{2,1,0:T(8,128)(2,1)} %bitcast.26), channel_id=1, source_target_pairs={{0,16},{8,24},{16,0},{24,8},{32,48},{40,56},{48,32},{56,40},{64,80... | collective-permute-start | bytes 393224 | tf_op jit(solution)/shard_map/ppermute | solution.py:339
  7.0 12.3 %collective-permute-start.1 = (bf16[8,128,128]{2,1,0:T(8,128)(2,1)S(1)}, bf16[8,128,128]{2,1,0:T(8,128)(2,1)S(1)}, u32[]{:S(2)}, u32[]{:S(2)}) collective-permute-start(bf16[8,128,128]{2,1,0:T(8,128)(2,1)S(1)} %pad_maximum_fusion.refs_0_), channel_id=1, source_target_pairs={{32,0},{40,8},{48,16},{56,24},{64,32},{72,40},{80,48},{88,56},{96,... | collective-permute-start | bytes 786440 | tf_op jit(solution)/shard_map/ppermute | solution.py:334
  11.3 8.5 %collective-permute-start.2 = (bf16[8,128,128]{2,1,0:T(8,128)(2,1)S(1)}, bf16[8,128,128]{2,1,0:T(8,128)(2,1)S(1)}, u32[]{:S(2)}, u32[]{:S(2)}) collective-permute-start(bf16[8,128,128]{2,1,0:T(8,128)(2,1)S(1)} %pad_maximum_fusion.refs_0_), channel_id=1, source_target_pairs={{0,32},{8,40},{16,48},{24,56},{32,64},{40,72},{48,80},{56,88},{64,... | collective-permute-start | bytes 786440 | tf_op jit(solution)/shard_map/ppermute | solution.py:334
  11.4 7.9 %copy-start = (bf16[1,1,736,128,128]{4,3,2,1,0:T(8,128)(2,1)S(1)}, bf16[1,1,736,128,128]{4,3,2,1,0:T(8,128)(2,1)}, u32[]{:S(2)}) copy-start(bf16[1,1,736,128,128]{4,3,2,1,0:T(8,128)(2,1)} %param.10) | copy-start | bytes 72351744
  19.9 8.1 %collective-permute-start.3 = (bf16[4,128,128]{2,1,0:T(8,128)(2,1)S(1)}, bf16[4,128,128]{2,1,0:T(8,128)(2,1)S(1)}, u32[]{:S(2)}, u32[]{:S(2)}) collective-permute-start(bf16[4,128,128]{2,1,0:T(8,128)(2,1)S(1)} %get-tuple-element.33), channel_id=1, source_target_pairs={{0,32},{8,40},{16,48},{24,56},{32,64},{40,72},{48,80},{56,88},{64,... | collective-permute-start | bytes 393224 | tf_op jit(solution)/shard_map/ppermute | solution.py:334
  20.0 8.1 %collective-permute-start.4 = (bf16[4,128,128]{2,1,0:T(8,128)(2,1)S(1)}, bf16[4,128,128]{2,1,0:T(8,128)(2,1)S(1)}, u32[]{:S(2)}, u32[]{:S(2)}) collective-permute-start(bf16[4,128,128]{2,1,0:T(8,128)(2,1)S(1)} %get-tuple-element.34), channel_id=1, source_target_pairs={{32,0},{40,8},{48,16},{56,24},{64,32},{72,40},{80,48},{88,56},{96,... | collective-permute-start | bytes 393224 | tf_op jit(solution)/shard_map/ppermute | solution.py:334
  23.2 4.8 %copy-start.1 = (bf16[512,128]{1,0:T(8,128)(2,1)S(1)}, bf16[512,128]{1,0:T(8,128)(2,1)}, u32[]{:S(2)}) copy-start(bf16[512,128]{1,0:T(8,128)(2,1)} %refs_3_.1) | copy-start | bytes 393220
  28.1 3.1 %collective-permute-start.5 = (bf16[32,128,128]{2,1,0:T(8,128)(2,1)S(1)}, bf16[32,128,128]{2,1,0:T(8,128)(2,1)S(1)}, u32[]{:S(2)}, u32[]{:S(2)}) collective-permute-start(bf16[32,128,128]{2,1,0:T(8,128)(2,1)S(1)} %get-tuple-element.35.refs_5_), channel_id=1, source_target_pairs={{0,8},{8,0},{16,24},{24,16},{32,40},{40,32},{48,56},{56,48},{64,72... | collective-permute-start | bytes 3145736 | tf_op jit(solution)/shard_map/ppermute | solution.py:339
  28.2 9.1 %collective-permute-start.6 = (bf16[4,128,128]{2,1,0:T(8,128)(2,1)S(1)}, bf16[4,128,128]{2,1,0:T(8,128)(2,1)S(1)}, u32[]{:S(2)}, u32[]{:S(2)}) collective-permute-start(bf16[4,128,128]{2,1,0:T(8,128)(2,1)S(1)} %get-tuple-element.37), channel_id=1, source_target_pairs={{0,4},{1,5},{2,6},{3,7},{4,0},{5,1},{6,2},{7,3},{8,12},{9,13},{10,... | collective-permute-start | bytes 393224 | tf_op jit(solution)/shard_map/ppermute | solution.py:339
  31.2 19.5 %slice-start = ((s8[24117248]{0:T(1024)(128)(4,1)}), s8[4194304]{0:T(1024)(128)(4,1)S(1)}, s32[]{:S(2)}) async-start(s8[24117248]{0:T(1024)(128)(4,1)} %bitcast.14), calls=%async_computation | async-start | bytes 8388608
  31.2 19.5 %slice-start.1 = ((s8[24117248]{0:T(1024)(128)(4,1)}), s8[4194304]{0:T(1024)(128)(4,1)S(1)}, s32[]{:S(2)}) async-start(s8[24117248]{0:T(1024)(128)(4,1)} %bitcast.14), calls=%async_computation.1 | async-start | bytes 8388608
  31.2 19.5 %slice-start.2 = ((s8[24117248]{0:T(1024)(128)(4,1)}), s8[4194304]{0:T(1024)(128)(4,1)S(1)}, s32[]{:S(2)}) async-start(s8[24117248]{0:T(1024)(128)(4,1)} %bitcast.14), calls=%async_computation.2 | async-start | bytes 8388608
  35.2 6.9 %collective-permute-start.8 = (bf16[8,128,128]{2,1,0:T(8,128)(2,1)S(1)}, bf16[8,128,128]{2,1,0:T(8,128)(2,1)S(1)}, u32[]{:S(2)}, u32[]{:S(2)}) collective-permute-start(bf16[8,128,128]{2,1,0:T(8,128)(2,1)S(1)} %get-tuple-element.41), channel_id=1, source_target_pairs={{1,0},{2,1},{3,2},{0,3},{5,4},{6,5},{7,6},{4,7},{9,8},{10,9},{11,1... | collective-permute-start | bytes 786440 | tf_op jit(solution)/shard_map/ppermute | solution.py:334
  35.5 15.2 %slice-start.3 = ((s8[24117248]{0:T(1024)(128)(4,1)}), s8[4194304]{0:T(1024)(128)(4,1)S(1)}, s32[]{:S(2)}) async-start(s8[24117248]{0:T(1024)(128)(4,1)} %bitcast.14), calls=%async_computation.3 | async-start | bytes 8388608
  35.5 15.2 %slice-start.4 = ((s8[24117248]{0:T(1024)(128)(4,1)}), s8[4194304]{0:T(1024)(128)(4,1)S(1)}, s32[]{:S(2)}) async-start(s8[24117248]{0:T(1024)(128)(4,1)} %bitcast.14), calls=%async_computation.4 | async-start | bytes 8388608
  35.5 15.2 %slice-start.5 = ((s8[24117248]{0:T(1024)(128)(4,1)}), s8[3145728]{0:T(1024)(128)(4,1)S(1)}, s32[]{:S(2)}) async-start(s8[24117248]{0:T(1024)(128)(4,1)} %bitcast.14), calls=%async_computation.5 | async-start | bytes 6291456
  35.5 8.9 %collective-permute-start.7 = (bf16[8,128,128]{2,1,0:T(8,128)(2,1)S(1)}, bf16[8,128,128]{2,1,0:T(8,128)(2,1)S(1)}, u32[]{:S(2)}, u32[]{:S(2)}) collective-permute-start(bf16[8,128,128]{2,1,0:T(8,128)(2,1)S(1)} %get-tuple-element.40), channel_id=1, source_target_pairs={{0,1},{1,2},{2,3},{3,0},{4,5},{5,6},{6,7},{7,4},{8,9},{9,10},{10,1... | collective-permute-start | bytes 786440 | tf_op jit(solution)/shard_map/ppermute | solution.py:334
  42.2 5.0 %collective-permute-start.10 = (bf16[4,128,128]{2,1,0:T(8,128)(2,1)S(1)}, bf16[4,128,128]{2,1,0:T(8,128)(2,1)S(1)}, u32[]{:S(2)}, u32[]{:S(2)}) collective-permute-start(bf16[4,128,128]{2,1,0:T(8,128)(2,1)S(1)} %add_convert_fusion.2), channel_id=1, source_target_pairs={{1,0},{2,1},{3,2},{0,3},{5,4},{6,5},{7,6},{4,7},{9,8},{10,9},{11,1... | collective-permute-start | bytes 393224 | tf_op jit(solution)/shard_map/ppermute | solution.py:334
  44.4 6.2 %collective-permute-start.9 = (bf16[4,128,128]{2,1,0:T(8,128)(2,1)S(1)}, bf16[4,128,128]{2,1,0:T(8,128)(2,1)S(1)}, u32[]{:S(2)}, u32[]{:S(2)}) collective-permute-start(bf16[4,128,128]{2,1,0:T(8,128)(2,1)S(1)} %add_convert_fusion.3), channel_id=1, source_target_pairs={{0,1},{1,2},{2,3},{3,0},{4,5},{5,6},{6,7},{7,4},{8,9},{9,10},{10,1... | collective-permute-start | bytes 393224 | tf_op jit(solution)/shard_map/ppermute | solution.py:334
  50.7 8.9 %copy-start.2 = (bf16[128,128]{1,0:T(8,128)(2,1)S(1)}, bf16[128,128]{1,0:T(8,128)(2,1)}, u32[]{:S(2)}) copy-start(bf16[128,128]{1,0:T(8,128)(2,1)} %refs_2_.1) | copy-start | bytes 98308
  51.7 8.0 %collective-permute-start.11 = (bf16[8,128,128]{2,1,0:T(8,128)(2,1)S(1)}, bf16[8,128,128]{2,1,0:T(8,128)(2,1)S(1)}, u32[]{:S(2)}, u32[]{:S(2)}) collective-permute-start(bf16[8,128,128]{2,1,0:T(8,128)(2,1)S(1)} %get-tuple-element.44.refs_0_), channel_id=1, source_target_pairs={{0,4},{1,5},{2,6},{3,7},{4,0},{5,1},{6,2},{7,3},{8,12},{9,13},{10,... | collective-permute-start | bytes 786440 | tf_op jit(solution)/shard_map/ppermute | solution.py:339
  60.9 8.5 %collective-permute-start.12 = (bf16[9,128,128]{2,1,0:T(8,128)(2,1)S(1)}, bf16[9,128,128]{2,1,0:T(8,128)(2,1)S(1)}, u32[]{:S(2)}, u32[]{:S(2)}) collective-permute-start(bf16[9,128,128]{2,1,0:T(8,128)(2,1)S(1)} %get-tuple-element.48.refs_5_.refs_8_), channel_id=1, source_target_pairs={{1,0},{2,1},{3,2},{0,3},{5,4},{6,5},{7,6},{4,7},{9,8},{10,9},{11,1... | collective-permute-start | bytes 884744 | tf_op jit(solution)/shard_map/ppermute | solution.py:334
  61.5 8.3 %collective-permute-start.13 = (bf16[9,128,128]{2,1,0:T(8,128)(2,1)S(1)}, bf16[9,128,128]{2,1,0:T(8,128)(2,1)S(1)}, u32[]{:S(2)}, u32[]{:S(2)}) collective-permute-start(bf16[9,128,128]{2,1,0:T(8,128)(2,1)S(1)} %get-tuple-element.48.refs_5_.refs_8_), channel_id=1, source_target_pairs={{0,1},{1,2},{2,3},{3,0},{4,5},{5,6},{6,7},{7,4},{8,9},{9,10},{10,1... | collective-permute-start | bytes 884744 | tf_op jit(solution)/shard_map/ppermute | solution.py:334
  69.4 7.2 %collective-permute-start.15 = (bf16[5,128,128]{2,1,0:T(8,128)(2,1)S(1)}, bf16[5,128,128]{2,1,0:T(8,128)(2,1)S(1)}, u32[]{:S(2)}, u32[]{:S(2)}) collective-permute-start(bf16[5,128,128]{2,1,0:T(8,128)(2,1)S(1)} %slice.27), channel_id=1, source_target_pairs={{1,0},{2,1},{3,2},{0,3},{5,4},{6,5},{7,6},{4,7},{9,8},{10,9},{11,1... | collective-permute-start | bytes 491528 | tf_op jit(solution)/shard_map/ppermute | solution.py:334
  69.8 6.7 %collective-permute-start.14 = (bf16[4,128,128]{2,1,0:T(8,128)(2,1)S(1)}, bf16[4,128,128]{2,1,0:T(8,128)(2,1)S(1)}, u32[]{:S(2)}, u32[]{:S(2)}) collective-permute-start(bf16[4,128,128]{2,1,0:T(8,128)(2,1)S(1)} %slice.26), channel_id=1, source_target_pairs={{0,1},{1,2},{2,3},{3,0},{4,5},{5,6},{6,7},{7,4},{8,9},{9,10},{10,1... | collective-permute-start | bytes 393224 | tf_op jit(solution)/shard_map/ppermute | solution.py:334
  79.2 4.0 %collective-permute-start.16 = (bf16[33,128,128]{2,1,0:T(8,128)(2,1)S(1)}, bf16[33,128,128]{2,1,0:T(8,128)(2,1)S(1)}, u32[]{:S(2)}, u32[]{:S(2)}) collective-permute-start(bf16[33,128,128]{2,1,0:T(8,128)(2,1)S(1)} %get-tuple-element.49), channel_id=1, source_target_pairs={{0,8},{8,0},{16,24},{24,16},{32,40},{40,32},{48,56},{56,48},{64,72... | collective-permute-start | bytes 3244040 | tf_op jit(solution)/shard_map/ppermute | solution.py:339
  83.4 13.1 %collective-permute-start.18 = (bf16[9,128,128]{2,1,0:T(8,128)(2,1)S(1)}, bf16[9,128,128]{2,1,0:T(8,128)(2,1)S(1)}, u32[]{:S(2)}, u32[]{:S(2)}) collective-permute-start(bf16[9,128,128]{2,1,0:T(8,128)(2,1)S(1)} %get-tuple-element.53), channel_id=1, source_target_pairs={{32,0},{40,8},{48,16},{56,24},{64,32},{72,40},{80,48},{88,56},{96,... | collective-permute-start | bytes 884744 | tf_op jit(solution)/shard_map/ppermute | solution.py:334
  85.7 10.7 %collective-permute-start.17 = (bf16[9,128,128]{2,1,0:T(8,128)(2,1)S(1)}, bf16[9,128,128]{2,1,0:T(8,128)(2,1)S(1)}, u32[]{:S(2)}, u32[]{:S(2)}) collective-permute-start(bf16[9,128,128]{2,1,0:T(8,128)(2,1)S(1)} %get-tuple-element.52.refs_5_), channel_id=1, source_target_pairs={{0,32},{8,40},{16,48},{24,56},{32,64},{40,72},{48,80},{56,88},{64,... | collective-permute-start | bytes 884744 | tf_op jit(solution)/shard_map/ppermute | solution.py:334
  96.4 7.6 %collective-permute-start.19 = (bf16[5,128,128]{2,1,0:T(8,128)(2,1)S(1)}, bf16[5,128,128]{2,1,0:T(8,128)(2,1)S(1)}, u32[]{:S(2)}, u32[]{:S(2)}) collective-permute-start(bf16[5,128,128]{2,1,0:T(8,128)(2,1)S(1)} %add_convert_fusion), channel_id=1, source_target_pairs={{0,32},{8,40},{16,48},{24,56},{32,64},{40,72},{48,80},{56,88},{64,... | collective-permute-start | bytes 491528 | tf_op jit(solution)/shard_map/ppermute | solution.py:334
  96.6 6.2 %collective-permute-start.20 = (bf16[4,128,128]{2,1,0:T(8,128)(2,1)S(1)}, bf16[4,128,128]{2,1,0:T(8,128)(2,1)S(1)}, u32[]{:S(2)}, u32[]{:S(2)}) collective-permute-start(bf16[4,128,128]{2,1,0:T(8,128)(2,1)S(1)} %add_convert_fusion.1), channel_id=1, source_target_pairs={{32,0},{40,8},{48,16},{56,24},{64,32},{72,40},{80,48},{88,56},{96,... | collective-permute-start | bytes 393224 | tf_op jit(solution)/shard_map/ppermute | solution.py:334
  104.1 5.6 %collective-permute-start.21 = (bf16[5,128,128]{2,1,0:T(8,128)(2,1)S(1)}, bf16[5,128,128]{2,1,0:T(8,128)(2,1)S(1)}, u32[]{:S(2)}, u32[]{:S(2)}) collective-permute-start(bf16[5,128,128]{2,1,0:T(8,128)(2,1)S(1)} %far_columns.1.refs_5_), channel_id=1, source_target_pairs={{0,16},{8,24},{16,0},{24,8},{32,48},{40,56},{48,32},{56,40},{64,80... | collective-permute-start | bytes 491528 | tf_op jit(solution)/shard_map/ppermute | solution.py:339

commit v3 on v2

--- a/solution.py
+++ b/solution.py
@@ -78,16 +78,24 @@
 def group_kernel(
     table_cuts, table_size, phase, first_key, pad, unroll, forward, n_extra, finish, *refs
 ):
-    bounds_ref, tile_ref, other_ref, key_ref, tiles_ref = refs[:5]
+    plan_refs, tiles_ref = refs[:4], refs[4]
     n_tables = len(table_cuts)
     table_refs = refs[5 : 5 + n_tables]
     extra_refs = refs[5 + n_tables : 5 + n_tables + n_extra]
-    out_refs = refs[5 + n_tables + n_extra : -2]
-    table, acc = refs[-2:]
+    out_refs = refs[5 + n_tables + n_extra : -7]
+    table, acc, bounds_ref, tile_ref, other_ref, key_ref, sems = refs[-7:]
+    copies = [
+        pltpu.make_async_copy(ref, here, sems.at[i])
+        for i, (ref, here) in enumerate(zip(plan_refs, (bounds_ref, tile_ref, other_ref, key_ref)))
+    ]
+    for copy in copies:
+        copy.start()
     for ref, (at, start, size) in zip(table_refs, table_cuts):
         table[at : at + size] = ref[start : start + size]
     table[table_size] = jnp.zeros((TS, TS), table.dtype)
     acc[...] = jnp.zeros_like(acc)
+    for copy in copies:
+        copy.wait()
 
     def product(group):
         picked = [tiles_ref[tile_ref[group * pad + i]] for i in range(pad)]
@@ -118,7 +126,7 @@
     plan, tiles, tables, table_size, phase, keys, pad, unroll, forward, extras, outs, finish, name
 ):
     bounds, tile_at, other_at, key_at = plan
-    scalar = pl.BlockSpec(memory_space=pltpu.SMEM)
+    anywhere = pl.BlockSpec(memory_space=pl.ANY)
     here = pl.BlockSpec(memory_space=pltpu.VMEM)
     n_keys = keys[1] - keys[0]
     share = tiles.shape[0] * n_keys // 64 if forward else tiles.shape[0] * n_keys // 96
@@ -136,11 +144,13 @@
             finish,
         ),
         out_shape=outs,
-        in_specs=[scalar] * 4 + [here] * (1 + len(tables) + len(extras)),
+        in_specs=[anywhere] * 4 + [here] * (1 + len(tables) + len(extras)),
         out_specs=[here] * len(outs),
         scratch_shapes=[
             pltpu.VMEM((table_size + 1, TS, TS), BF16),
             pltpu.VMEM((n_keys, TS, TS), F32),
+            *[pltpu.SMEM(part.shape, part.dtype) for part in plan],
+            pltpu.SemaphoreType.DMA((4,)),
         ],
         compiler_params=pltpu.CompilerParams(vmem_limit_bytes=VMEM_LIMIT),
         cost_estimate=pl.CostEstimate(
@@ -341,7 +351,8 @@
 
 def local(features, weight, cotangent, tiles, tile_rows, tile_cols, tile_counts):
     gr, gc = lax.axis_index("gr"), lax.axis_index("gc")
-    rows, cols = tile_rows[0, 0], tile_cols[0, 0]
+    both = (tile_rows * 64 + tile_cols)[0, 0]
+    rows, cols = both >> 6, both & 63
     live = jnp.arange(rows.shape[0], dtype=jnp.int32) < tile_counts[0, 0]
     sent, arrived = places(ORDER), places(ARRIVAL)
 
@@ -363,7 +374,8 @@
     x_up, x_down = ring_permutes("gc")
 
     own = features.reshape(4, TS, TS)
-    pair = jnp.concatenate([own, y_swap(own)], 0)
+    far = y_swap(own)
+    pair = jnp.concatenate([join("own_block", own), far], 0)
     previous, following = z_up(pair), z_down(pair)
     blocks = pltpu.with_memory_space_constraint(tiles[0, 0], pltpu.VMEM)
     held = call(join_kernel, array(8), "after_tiles", blocks, pair)

time: 111 us -> 109 us (0.982)
  Pallas kernels: 29.9 us -> 16.2 us
  waiting for transfers between devices: 35.3 us -> 43.2 us
  starting transfers between devices: 29.9 us -> 34.5 us
  other arithmetic: 5.86 us -> 4.29 us
    pallas_call x7, Pallas kernels: 27.4 us -> 13.7 us  [group_pass(): pl.pallas_call(functools.partial(group_kernel, tuple((t[1:] for t in tabl...]
    ppermute x8, starting transfers between devices: 16.5 us -> 22.2 us  [ring_permutes(): lax.ppermute(v, axis, down)]
    ppermute x8, waiting for transfers between devices: 12.7 us -> 16.1 us  [ring_permutes(): lax.ppermute(v, axis, up)]
    ppermute x6, waiting for transfers between devices: 9.8 us -> 12.2 us  [pair_permute(): lax.ppermute(value, axis, [(i, i ^ mask) for i in range(size)])]
    ppermute x8, waiting for transfers between devices: 12.8 us -> 14.9 us  [ring_permutes(): lax.ppermute(v, axis, down)]
    unnamed x18 -> x20, local copies, waits for them, and re-layouts: 7.89 us -> 8.79 us
  transfers between devices with their start and end apart: 22 -> 22, of which waited for: 10 -> 14; matrix products, arithmetic and copies ran while one was open for 4% -> 3% of each run, Pallas kernels for 22% -> 11%
where the time goes in v3:
time: 109 us
  waiting for transfers between devices  43.2 us (40%)
  starting transfers between devices  34.5 us (32%)
  Pallas kernels  16.2 us (15%)
  local copies, waits for them, and re-layouts  8.81 us (8%)
  other arithmetic  4.29 us (4%)
  between operations  1.67 us (2%)
    ppermute x8, starting transfers between devices, ring_permutes(): lax.ppermute(v, axis, down)  22.2 us
    ppermute x8, waiting for transfers between devices, ring_permutes(): lax.ppermute(v, axis, up)  16.1 us
    ppermute x8, waiting for transfers between devices, ring_permutes(): lax.ppermute(v, axis, down)  14.9 us
    pallas_call x7, Pallas kernels, group_pass(): pl.pallas_call(functools.partial(group_kernel, tuple((t[1:] for t in tabl...  13.7 us
    ppermute x6, waiting for transfers between devices, pair_permute(): lax.ppermute(value, axis, [(i, i ^ mask) for i in range(size)])  12.2 us
    unnamed x20, local copies, waits for them, and re-layouts  8.79 us
    ppermute x6, starting transfers between devices, pair_permute(): lax.ppermute(value, axis, [(i, i ^ mask) for i in range(size)])  7.61 us
    ppermute x8, starting transfers between devices, ring_permutes(): lax.ppermute(v, axis, up)  4.65 us
  transfers between devices with their start and end apart: 22, of which 14 were waited for; matrix products, arithmetic and copies ran while one was open for 3% of the time, Pallas kernels for 11%

profile of v3, /device:TPU:0, one launch (start us, length us, event | category | flops | bytes accessed | tf_op | source)
XLA Modules:
  0.0 108.7 jit_solution(463225285002799883)
XLA Ops:
  0.6 1.7 %collective-permute-start = (bf16[4,128,128]{2,1,0:T(8,128)(2,1)}, bf16[4,128,128]{2,1,0:T(8,128)(2,1)S(1)}, u32[]{:S(2)}, u32[]{:S(2)}) collective-permute-start(bf16[4,128,128]{2,1,0:T(8,128)(2,1)} %bitcast.26), channel_id=1, source_target_pairs={{0,16},{8,24},{16,0},{24,8},{32,48},{40,56},{48,32},{56,40},{64,80... | collective-permute-start | bytes 393224 | tf_op jit(solution)/shard_map/ppermute | solution.py:349
  2.4 0.8 multiply_reduce_fusion
  4.1 0.2 select_reduce_fusion.5
  4.3 0.4 convert_reduce_fusion.1
  5.0 0.9 copy-done.2
  5.9 0.4 select_reduce_fusion.1
  6.3 4.1 %collective-permute-start.1 = (bf16[8,128,128]{2,1,0:T(8,128)(2,1)S(1)}, bf16[8,128,128]{2,1,0:T(8,128)(2,1)S(1)}, u32[]{:S(2)}, u32[]{:S(2)}) collective-permute-start(bf16[8,128,128]{2,1,0:T(8,128)(2,1)S(1)} %pad_maximum_fusion.refs_0_), channel_id=1, source_target_pairs={{32,0},{40,8},{48,16},{56,24},{64,32},{72,40},{80,48},{88,56},{96,... | collective-permute-start | bytes 786440 | tf_op jit(solution)/shard_map/ppermute | solution.py:344
  10.6 7.8 %copy-done = bf16[1,1,736,128,128]{4,3,2,1,0:T(8,128)(2,1)S(1)} copy-done((bf16[1,1,736,128,128]{4,3,2,1,0:T(8,128)(2,1)S(1)}, bf16[1,1,736,128,128]{4,3,2,1,0:T(8,128)(2,1)}, u32[]{:S(2)}) %copy-start) | copy-done | bytes 24117272
  18.5 0.7 collective-permute-done.2.refs_2_
  19.3 3.2 %collective-permute-start.4 = (bf16[4,128,128]{2,1,0:T(8,128)(2,1)S(1)}, bf16[4,128,128]{2,1,0:T(8,128)(2,1)S(1)}, u32[]{:S(2)}, u32[]{:S(2)}) collective-permute-start(bf16[4,128,128]{2,1,0:T(8,128)(2,1)S(1)} %get-tuple-element.34), channel_id=1, source_target_pairs={{32,0},{40,8},{48,16},{56,24},{64,32},{72,40},{80,48},{88,56},{96,... | collective-permute-start | bytes 393224 | tf_op jit(solution)/shard_map/ppermute | solution.py:344
  22.6 2.4 %forward_early.1 = (f32[32,128,128]{2,1,0:T(8,128)S(1)}, bf16[24,128,128]{2,1,0:T(8,128)(2,1)S(1)}) custom-call(s32[4]{0:T(128)S(1)} %select_reduce_fusion.10.refs_0_, s32[1024]{0:T(1024)S(1)} %get-tuple-element.74.refs_1_, s32[1024]{0:T(1024)S(1)} %get-tuple-element.73.refs_2_, s32[512]{0:T(512)S(1)} %broadcast_add_fusion.1.refs_3_, ...), custom_call_target="tpu_custom_call" | custom-call | flops 12348030976 | bytes 4194304 | tf_op jit(solution)/shard_map/forward_early/pallas_call | solution.py:133
  25.0 0.5 collective-permute-done.3.refs_1_
  25.7 3.0 %collective-permute-start.6 = (bf16[4,128,128]{2,1,0:T(8,128)(2,1)S(1)}, bf16[4,128,128]{2,1,0:T(8,128)(2,1)S(1)}, u32[]{:S(2)}, u32[]{:S(2)}) collective-permute-start(bf16[4,128,128]{2,1,0:T(8,128)(2,1)S(1)} %get-tuple-element.37), channel_id=1, source_target_pairs={{0,4},{1,5},{2,6},{3,7},{4,0},{5,1},{6,2},{7,3},{8,12},{9,13},{10,... | collective-permute-start | bytes 393224 | tf_op jit(solution)/shard_map/ppermute | solution.py:349
  28.7 1.6 %forward_sent.1 = (bf16[8,128,128]{2,1,0:T(8,128)(2,1)S(1)}, bf16[8,128,128]{2,1,0:T(8,128)(2,1)S(1)}) custom-call(s32[4]{0:T(128)S(1)} %select_reduce_fusion.10.refs_0_, s32[1024]{0:T(1024)S(1)} %get-tuple-element.74.refs_1_, s32[1024]{0:T(1024)S(1)} %get-tuple-element.73.refs_2_, s32[512]{0:T(512)S(1)} %broadcast_add_fusion.1.refs_3_, ...), custom_call_target="tpu_custom_call" | custom-call | flops 6174015488 | bytes 4194304 | tf_op jit(solution)/shard_map/forward_sent/pallas_call | solution.py:133
  30.3 3.9 %collective-permute-start.8 = (bf16[8,128,128]{2,1,0:T(8,128)(2,1)S(1)}, bf16[8,128,128]{2,1,0:T(8,128)(2,1)S(1)}, u32[]{:S(2)}, u32[]{:S(2)}) collective-permute-start(bf16[8,128,128]{2,1,0:T(8,128)(2,1)S(1)} %get-tuple-element.41), channel_id=1, source_target_pairs={{1,0},{2,1},{3,2},{0,3},{5,4},{6,5},{7,6},{4,7},{9,8},{10,9},{11,1... | collective-permute-start | bytes 786440 | tf_op jit(solution)/shard_map/ppermute | solution.py:344
  34.1 1.8 %collective-permute-start.7 = (bf16[8,128,128]{2,1,0:T(8,128)(2,1)S(1)}, bf16[8,128,128]{2,1,0:T(8,128)(2,1)S(1)}, u32[]{:S(2)}, u32[]{:S(2)}) collective-permute-start(bf16[8,128,128]{2,1,0:T(8,128)(2,1)S(1)} %get-tuple-element.40), channel_id=1, source_target_pairs={{0,1},{1,2},{2,3},{3,0},{4,5},{5,6},{6,7},{7,4},{8,9},{9,10},{10,1... | collective-permute-start | bytes 786440 | tf_op jit(solution)/shard_map/ppermute | solution.py:344
  36.0 2.3 %forward_kept.1 = (bf16[4,128,128]{2,1,0:T(8,128)(2,1)S(1)}, bf16[4,128,128]{2,1,0:T(8,128)(2,1)S(1)}, f32[4,128,128]{2,1,0:T(8,128)S(1)}, f32[4,128,128]{2,1,0:T(8,128)S(1)}) custom-call(s32[4]{0:T(128)S(1)} %select_reduce_fusion.10.refs_0_, s32[1024]{0:T(1024)S(1)} %get-tuple-element.74.refs_1_, s32[1024]{0:T(1024)S(1)} %get-tuple-element.73.refs_2_, ...), custom_call_target="tpu_custom_call" | custom-call | flops 6174015488 | bytes 4194304 | tf_op jit(solution)/shard_map/forward_kept/pallas_call | solution.py:133
  38.3 4.2 %collective-permute-done.8.refs_3_ = bf16[8,128,128]{2,1,0:T(8,128)(2,1)S(1)} collective-permute-done((bf16[8,128,128]{2,1,0:T(8,128)(2,1)S(1)}, bf16[8,128,128]{2,1,0:T(8,128)(2,1)S(1)}, u32[]{:S(2)}, u32[]{:S(2)}) %collective-permute-start.8) | collective-permute-done | bytes 262176 | tf_op jit(solution)/shard_map/ppermute | solution.py:344
  42.5 1.5 %collective-permute-start.10 = (bf16[4,128,128]{2,1,0:T(8,128)(2,1)S(1)}, bf16[4,128,128]{2,1,0:T(8,128)(2,1)S(1)}, u32[]{:S(2)}, u32[]{:S(2)}) collective-permute-start(bf16[4,128,128]{2,1,0:T(8,128)(2,1)S(1)} %add_convert_fusion.2), channel_id=1, source_target_pairs={{1,0},{2,1},{3,2},{0,3},{5,4},{6,5},{7,6},{4,7},{9,8},{10,9},{11,1... | collective-permute-start | bytes 393224 | tf_op jit(solution)/shard_map/ppermute | solution.py:344
  44.0 0.2 collective-permute-done.7.refs_2_
  44.2 0.5 collective-permute-start.9
  44.7 2.9 %collective-permute-done.10.refs_5_ = bf16[4,128,128]{2,1,0:T(8,128)(2,1)S(1)} collective-permute-done((bf16[4,128,128]{2,1,0:T(8,128)(2,1)S(1)}, bf16[4,128,128]{2,1,0:T(8,128)(2,1)S(1)}, u32[]{:S(2)}, u32[]{:S(2)}) %collective-permute-start.10) | collective-permute-done | bytes 131104 | tf_op jit(solution)/shard_map/ppermute | solution.py:344
  47.6 3.4 %collective-permute-done.9.refs_4_ = bf16[4,128,128]{2,1,0:T(8,128)(2,1)S(1)} collective-permute-done((bf16[4,128,128]{2,1,0:T(8,128)(2,1)S(1)}, bf16[4,128,128]{2,1,0:T(8,128)(2,1)S(1)}, u32[]{:S(2)}, u32[]{:S(2)}) %collective-permute-start.9) | collective-permute-done | bytes 131104 | tf_op jit(solution)/shard_map/ppermute | solution.py:344
  51.5 0.2 select_reduce_fusion.4
  51.7 0.4 convert_reduce_fusion
  52.1 2.6 %collective-permute-start.11 = (bf16[8,128,128]{2,1,0:T(8,128)(2,1)S(1)}, bf16[8,128,128]{2,1,0:T(8,128)(2,1)S(1)}, u32[]{:S(2)}, u32[]{:S(2)}) collective-permute-start(bf16[8,128,128]{2,1,0:T(8,128)(2,1)S(1)} %get-tuple-element.44.refs_0_), channel_id=1, source_target_pairs={{0,4},{1,5},{2,6},{3,7},{4,0},{5,1},{6,2},{7,3},{8,12},{9,13},{10,... | collective-permute-start | bytes 786440 | tf_op jit(solution)/shard_map/ppermute | solution.py:349
  54.9 0.5 select_reduce_fusion
  55.5 5.8 %collective-permute-done.11.refs_1_ = bf16[8,128,128]{2,1,0:T(8,128)(2,1)S(1)} collective-permute-done((bf16[8,128,128]{2,1,0:T(8,128)(2,1)S(1)}, bf16[8,128,128]{2,1,0:T(8,128)(2,1)S(1)}, u32[]{:S(2)}, u32[]{:S(2)}) %collective-permute-start.11) | collective-permute-done | bytes 262176 | tf_op jit(solution)/shard_map/ppermute | solution.py:349
  61.3 1.3 %middle.1 = (bf16[512,128]{1,0:T(8,128)(2,1)}, bf16[9,128,128]{2,1,0:T(8,128)(2,1)S(1)}) custom-call(bf16[736,128,128]{2,1,0:T(8,128)(2,1)S(1)} %bitcast.17, bf16[8,128,128]{2,1,0:T(8,128)(2,1)S(1)} %get-tuple-element.44.refs_0_, bf16[8,128,128]{2,1,0:T(8,128)(2,1)S(1)} %collective-permute-done.11.refs_1_, bf16[128,128]{1,0:T(8,128)(2,1)S(1)} %copy-done.3, ...), custom_call_target="tpu_custom_call" | custom-call | tf_op jit(solution)/shard_map/middle/pallas_call | solution.py:218
  62.5 0.2 collective-permute-start.12
  62.8 1.8 %collective-permute-start.13 = (bf16[9,128,128]{2,1,0:T(8,128)(2,1)S(1)}, bf16[9,128,128]{2,1,0:T(8,128)(2,1)S(1)}, u32[]{:S(2)}, u32[]{:S(2)}) collective-permute-start(bf16[9,128,128]{2,1,0:T(8,128)(2,1)S(1)} %get-tuple-element.48.refs_5_.refs_8_), channel_id=1, source_target_pairs={{0,1},{1,2},{2,3},{3,0},{4,5},{5,6},{6,7},{7,4},{8,9},{9,10},{10,1... | collective-permute-start | bytes 884744 | tf_op jit(solution)/shard_map/ppermute | solution.py:344
  64.7 5.3 %collective-permute-done.12.refs_6_.refs_9_ = bf16[9,128,128]{2,1,0:T(8,128)(2,1)S(1)} collective-permute-done((bf16[9,128,128]{2,1,0:T(8,128)(2,1)S(1)}, bf16[9,128,128]{2,1,0:T(8,128)(2,1)S(1)}, u32[]{:S(2)}, u32[]{:S(2)}) %collective-permute-start.12) | collective-permute-done | bytes 294944 | tf_op jit(solution)/shard_map/ppermute | solution.py:344
  70.0 1.9 %collective-permute-start.15 = (bf16[5,128,128]{2,1,0:T(8,128)(2,1)S(1)}, bf16[5,128,128]{2,1,0:T(8,128)(2,1)S(1)}, u32[]{:S(2)}, u32[]{:S(2)}) collective-permute-start(bf16[5,128,128]{2,1,0:T(8,128)(2,1)S(1)} %slice.27), channel_id=1, source_target_pairs={{1,0},{2,1},{3,2},{0,3},{5,4},{6,5},{7,6},{4,7},{9,8},{10,9},{11,1... | collective-permute-start | bytes 491528 | tf_op jit(solution)/shard_map/ppermute | solution.py:344
  71.9 0.4 collective-permute-start.14
  72.4 2.4 %backward_early.1.refs_7_ = f32[32,128,128]{2,1,0:T(8,128)S(1)} custom-call(s32[5]{0:T(128)S(1)} %select_reduce_fusion.7.refs_0_, s32[1088]{0:T(1024)S(1)} %get-tuple-element.70.refs_1_, s32[1088]{0:T(1024)S(1)} %get-tuple-element.69.refs_2_, s32[544]{0:T(1024)S(1)} %broadcast_add_fusion.refs_3_, bf16[736,128,128]{2,1,0:T(8,128)(2,1)S(1)} %bitcast.18, ...), custom_call_target="tpu_custom_call" | custom-call | flops 8220835840 | bytes 4194304 | tf_op jit(solution)/shard_map/backward_early/pallas_call | solution.py:133
  74.8 3.4 %collective-permute-done.14.refs_5_.refs_8_ = bf16[4,128,128]{2,1,0:T(8,128)(2,1)S(1)} collective-permute-done((bf16[4,128,128]{2,1,0:T(8,128)(2,1)S(1)}, bf16[4,128,128]{2,1,0:T(8,128)(2,1)S(1)}, u32[]{:S(2)}, u32[]{:S(2)}) %collective-permute-start.14) | collective-permute-done | bytes 131104 | tf_op jit(solution)/shard_map/ppermute | solution.py:344
  78.2 1.7 %backward_theirs.1 = (bf16[33,128,128]{2,1,0:T(8,128)(2,1)S(1)}, bf16[1,128,128]{2,1,0:T(8,128)(2,1)S(1)}) custom-call(s32[5]{0:T(128)S(1)} %select_reduce_fusion.7.refs_0_, s32[1088]{0:T(1024)S(1)} %get-tuple-element.70.refs_1_, s32[1088]{0:T(1024)S(1)} %get-tuple-element.69.refs_2_, s32[544]{0:T(1024)S(1)} %broadcast_add_fusion.refs_3_, ...), custom_call_target="tpu_custom_call" | custom-call | flops 8220835840 | bytes 4194304 | tf_op jit(solution)/shard_map/backward_theirs/pallas_call | solution.py:133
  80.0 1.6 %backward_sent.1.refs_0_ = bf16[16,128,128]{2,1,0:T(8,128)(2,1)S(1)} custom-call(s32[5]{0:T(128)S(1)} %select_reduce_fusion.7.refs_0_, s32[1088]{0:T(1024)S(1)} %get-tuple-element.70.refs_1_, s32[1088]{0:T(1024)S(1)} %get-tuple-element.69.refs_2_, s32[544]{0:T(1024)S(1)} %broadcast_add_fusion.refs_3_, bf16[736,128,128]{2,1,0:T(8,128)(2,1)S(1)} %bitcast.20, ...), custom_call_target="tpu_custom_call" | custom-call | flops 4093640704 | bytes 4194304 | tf_op jit(solution)/shard_map/backward_sent/pallas_call | solution.py:133
  81.6 1.1 %collective-permute-done.16.refs_10_.refs_1_ = bf16[33,128,128]{2,1,0:T(8,128)(2,1)S(1)} collective-permute-done((bf16[33,128,128]{2,1,0:T(8,128)(2,1)S(1)}, bf16[33,128,128]{2,1,0:T(8,128)(2,1)S(1)}, u32[]{:S(2)}, u32[]{:S(2)}) %collective-permute-start.16) | collective-permute-done | bytes 1081376 | tf_op jit(solution)/shard_map/ppermute | solution.py:349
  82.7 0.1 add_core.1
  82.8 4.1 %collective-permute-start.18 = (bf16[9,128,128]{2,1,0:T(8,128)(2,1)S(1)}, bf16[9,128,128]{2,1,0:T(8,128)(2,1)S(1)}, u32[]{:S(2)}, u32[]{:S(2)}) collective-permute-start(bf16[9,128,128]{2,1,0:T(8,128)(2,1)S(1)} %get-tuple-element.53), channel_id=1, source_target_pairs={{32,0},{40,8},{48,16},{56,24},{64,32},{72,40},{80,48},{88,56},{96,... | collective-permute-start | bytes 884744 | tf_op jit(solution)/shard_map/ppermute | solution.py:344
  87.0 1.6 %backward_kept.1 = (bf16[5,128,128]{2,1,0:T(8,128)(2,1)S(1)}, bf16[4,128,128]{2,1,0:T(8,128)(2,1)S(1)}, f32[4,128,128]{2,1,0:T(8,128)S(1)}, f32[4,128,128]{2,1,0:T(8,128)S(1)}) custom-call(s32[5]{0:T(128)S(1)} %select_reduce_fusion.7.refs_0_, s32[1088]{0:T(1024)S(1)} %get-tuple-element.70.refs_1_, s32[1088]{0:T(1024)S(1)} %get-tuple-element.69.refs_2_, ...), custom_call_target="tpu_custom_call" | custom-call | flops 4093640704 | bytes 4194304 | tf_op jit(solution)/shard_map/backward_kept/pallas_call | solution.py:133
  88.6 7.2 %collective-permute-done.17.refs_1_ = bf16[9,128,128]{2,1,0:T(8,128)(2,1)S(1)} collective-permute-done((bf16[9,128,128]{2,1,0:T(8,128)(2,1)S(1)}, bf16[9,128,128]{2,1,0:T(8,128)(2,1)S(1)}, u32[]{:S(2)}, u32[]{:S(2)}) %collective-permute-start.17) | collective-permute-done | bytes 294944 | tf_op jit(solution)/shard_map/ppermute | solution.py:344
  96.0 3.3 %collective-permute-start.20 = (bf16[4,128,128]{2,1,0:T(8,128)(2,1)S(1)}, bf16[4,128,128]{2,1,0:T(8,128)(2,1)S(1)}, u32[]{:S(2)}, u32[]{:S(2)}) collective-permute-start(bf16[4,128,128]{2,1,0:T(8,128)(2,1)S(1)} %add_convert_fusion.1), channel_id=1, source_target_pairs={{32,0},{40,8},{48,16},{56,24},{64,32},{72,40},{80,48},{88,56},{96,... | collective-permute-start | bytes 393224 | tf_op jit(solution)/shard_map/ppermute | solution.py:344
  99.3 2.5 %collective-permute-done.20.refs_4_ = bf16[4,128,128]{2,1,0:T(8,128)(2,1)S(1)} collective-permute-done((bf16[4,128,128]{2,1,0:T(8,128)(2,1)S(1)}, bf16[4,128,128]{2,1,0:T(8,128)(2,1)S(1)}, u32[]{:S(2)}, u32[]{:S(2)}) %collective-permute-start.20) | collective-permute-done | bytes 131104 | tf_op jit(solution)/shard_map/ppermute | solution.py:344
  101.8 0.7 collective-permute-done.19.refs_3_
  102.6 5.3 %collective-permute-done.21.refs_6_ = bf16[5,128,128]{2,1,0:T(8,128)(2,1)S(1)} collective-permute-done((bf16[5,128,128]{2,1,0:T(8,128)(2,1)S(1)}, bf16[5,128,128]{2,1,0:T(8,128)(2,1)S(1)}, u32[]{:S(2)}, u32[]{:S(2)}) %collective-permute-start.21) | collective-permute-done | bytes 163872 | tf_op jit(solution)/shard_map/ppermute | solution.py:349
  107.9 0.8 last.1
  (77 shorter events, 2.5 us)
Async XLA Ops:
  0.6 5.7 %collective-permute-start = (bf16[4,128,128]{2,1,0:T(8,128)(2,1)}, bf16[4,128,128]{2,1,0:T(8,128)(2,1)S(1)}, u32[]{:S(2)}, u32[]{:S(2)}) collective-permute-start(bf16[4,128,128]{2,1,0:T(8,128)(2,1)} %bitcast.26), channel_id=1, source_target_pairs={{0,16},{8,24},{16,0},{24,8},{32,48},{40,56},{48,32},{56,40},{64,80... | collective-permute-start | bytes 393224 | tf_op jit(solution)/shard_map/ppermute | solution.py:349
  5.0 0.9 copy-start.2
  6.3 12.1 %collective-permute-start.1 = (bf16[8,128,128]{2,1,0:T(8,128)(2,1)S(1)}, bf16[8,128,128]{2,1,0:T(8,128)(2,1)S(1)}, u32[]{:S(2)}, u32[]{:S(2)}) collective-permute-start(bf16[8,128,128]{2,1,0:T(8,128)(2,1)S(1)} %pad_maximum_fusion.refs_0_), channel_id=1, source_target_pairs={{32,0},{40,8},{48,16},{56,24},{64,32},{72,40},{80,48},{88,56},{96,... | collective-permute-start | bytes 786440 | tf_op jit(solution)/shard_map/ppermute | solution.py:344
  10.5 8.7 %collective-permute-start.2 = (bf16[8,128,128]{2,1,0:T(8,128)(2,1)S(1)}, bf16[8,128,128]{2,1,0:T(8,128)(2,1)S(1)}, u32[]{:S(2)}, u32[]{:S(2)}) collective-permute-start(bf16[8,128,128]{2,1,0:T(8,128)(2,1)S(1)} %pad_maximum_fusion.refs_0_), channel_id=1, source_target_pairs={{0,32},{8,40},{16,48},{24,56},{32,64},{40,72},{48,80},{56,88},{64,... | collective-permute-start | bytes 786440 | tf_op jit(solution)/shard_map/ppermute | solution.py:344
  10.6 7.9 %copy-start = (bf16[1,1,736,128,128]{4,3,2,1,0:T(8,128)(2,1)S(1)}, bf16[1,1,736,128,128]{4,3,2,1,0:T(8,128)(2,1)}, u32[]{:S(2)}) copy-start(bf16[1,1,736,128,128]{4,3,2,1,0:T(8,128)(2,1)} %param.10) | copy-start | bytes 72351744
  19.2 6.2 %collective-permute-start.3 = (bf16[4,128,128]{2,1,0:T(8,128)(2,1)S(1)}, bf16[4,128,128]{2,1,0:T(8,128)(2,1)S(1)}, u32[]{:S(2)}, u32[]{:S(2)}) collective-permute-start(bf16[4,128,128]{2,1,0:T(8,128)(2,1)S(1)} %get-tuple-element.33), channel_id=1, source_target_pairs={{0,32},{8,40},{16,48},{24,56},{32,64},{40,72},{48,80},{56,88},{64,... | collective-permute-start | bytes 393224 | tf_op jit(solution)/shard_map/ppermute | solution.py:344
  19.3 6.2 %collective-permute-start.4 = (bf16[4,128,128]{2,1,0:T(8,128)(2,1)S(1)}, bf16[4,128,128]{2,1,0:T(8,128)(2,1)S(1)}, u32[]{:S(2)}, u32[]{:S(2)}) collective-permute-start(bf16[4,128,128]{2,1,0:T(8,128)(2,1)S(1)} %get-tuple-element.34), channel_id=1, source_target_pairs={{32,0},{40,8},{48,16},{56,24},{64,32},{72,40},{80,48},{88,56},{96,... | collective-permute-start | bytes 393224 | tf_op jit(solution)/shard_map/ppermute | solution.py:344
  22.5 2.9 %copy-start.1 = (bf16[512,128]{1,0:T(8,128)(2,1)S(1)}, bf16[512,128]{1,0:T(8,128)(2,1)}, u32[]{:S(2)}) copy-start(bf16[512,128]{1,0:T(8,128)(2,1)} %refs_3_.1) | copy-start | bytes 393220
  25.6 3.1 %collective-permute-start.5 = (bf16[32,128,128]{2,1,0:T(8,128)(2,1)S(1)}, bf16[32,128,128]{2,1,0:T(8,128)(2,1)S(1)}, u32[]{:S(2)}, u32[]{:S(2)}) collective-permute-start(bf16[32,128,128]{2,1,0:T(8,128)(2,1)S(1)} %get-tuple-element.35.refs_5_), channel_id=1, source_target_pairs={{0,8},{8,0},{16,24},{24,16},{32,40},{40,32},{48,56},{56,48},{64,72... | collective-permute-start | bytes 3145736 | tf_op jit(solution)/shard_map/ppermute | solution.py:349
  25.7 10.3 %collective-permute-start.6 = (bf16[4,128,128]{2,1,0:T(8,128)(2,1)S(1)}, bf16[4,128,128]{2,1,0:T(8,128)(2,1)S(1)}, u32[]{:S(2)}, u32[]{:S(2)}) collective-permute-start(bf16[4,128,128]{2,1,0:T(8,128)(2,1)S(1)} %get-tuple-element.37), channel_id=1, source_target_pairs={{0,4},{1,5},{2,6},{3,7},{4,0},{5,1},{6,2},{7,3},{8,12},{9,13},{10,... | collective-permute-start | bytes 393224 | tf_op jit(solution)/shard_map/ppermute | solution.py:349
  28.7 22.4 %slice-start = ((s8[24117248]{0:T(1024)(128)(4,1)}), s8[4194304]{0:T(1024)(128)(4,1)S(1)}, s32[]{:S(2)}) async-start(s8[24117248]{0:T(1024)(128)(4,1)} %bitcast.14), calls=%async_computation | async-start | bytes 8388608
  28.7 22.4 %slice-start.1 = ((s8[24117248]{0:T(1024)(128)(4,1)}), s8[4194304]{0:T(1024)(128)(4,1)S(1)}, s32[]{:S(2)}) async-start(s8[24117248]{0:T(1024)(128)(4,1)} %bitcast.14), calls=%async_computation.1 | async-start | bytes 8388608
  28.7 22.4 %slice-start.2 = ((s8[24117248]{0:T(1024)(128)(4,1)}), s8[4194304]{0:T(1024)(128)(4,1)S(1)}, s32[]{:S(2)}) async-start(s8[24117248]{0:T(1024)(128)(4,1)} %bitcast.14), calls=%async_computation.2 | async-start | bytes 8388608
  30.3 12.2 %collective-permute-start.8 = (bf16[8,128,128]{2,1,0:T(8,128)(2,1)S(1)}, bf16[8,128,128]{2,1,0:T(8,128)(2,1)S(1)}, u32[]{:S(2)}, u32[]{:S(2)}) collective-permute-start(bf16[8,128,128]{2,1,0:T(8,128)(2,1)S(1)} %get-tuple-element.41), channel_id=1, source_target_pairs={{1,0},{2,1},{3,2},{0,3},{5,4},{6,5},{7,6},{4,7},{9,8},{10,9},{11,1... | collective-permute-start | bytes 786440 | tf_op jit(solution)/shard_map/ppermute | solution.py:344
  34.1 17.0 %slice-start.3 = ((s8[24117248]{0:T(1024)(128)(4,1)}), s8[4194304]{0:T(1024)(128)(4,1)S(1)}, s32[]{:S(2)}) async-start(s8[24117248]{0:T(1024)(128)(4,1)} %bitcast.14), calls=%async_computation.3 | async-start | bytes 8388608
  34.1 17.0 %slice-start.4 = ((s8[24117248]{0:T(1024)(128)(4,1)}), s8[4194304]{0:T(1024)(128)(4,1)S(1)}, s32[]{:S(2)}) async-start(s8[24117248]{0:T(1024)(128)(4,1)} %bitcast.14), calls=%async_computation.4 | async-start | bytes 8388608
  34.1 17.0 %slice-start.5 = ((s8[24117248]{0:T(1024)(128)(4,1)}), s8[3145728]{0:T(1024)(128)(4,1)S(1)}, s32[]{:S(2)}) async-start(s8[24117248]{0:T(1024)(128)(4,1)} %bitcast.14), calls=%async_computation.5 | async-start | bytes 6291456
  34.1 10.1 %collective-permute-start.7 = (bf16[8,128,128]{2,1,0:T(8,128)(2,1)S(1)}, bf16[8,128,128]{2,1,0:T(8,128)(2,1)S(1)}, u32[]{:S(2)}, u32[]{:S(2)}) collective-permute-start(bf16[8,128,128]{2,1,0:T(8,128)(2,1)S(1)} %get-tuple-element.40), channel_id=1, source_target_pairs={{0,1},{1,2},{2,3},{3,0},{4,5},{5,6},{6,7},{7,4},{8,9},{9,10},{10,1... | collective-permute-start | bytes 786440 | tf_op jit(solution)/shard_map/ppermute | solution.py:344
  42.5 5.1 %collective-permute-start.10 = (bf16[4,128,128]{2,1,0:T(8,128)(2,1)S(1)}, bf16[4,128,128]{2,1,0:T(8,128)(2,1)S(1)}, u32[]{:S(2)}, u32[]{:S(2)}) collective-permute-start(bf16[4,128,128]{2,1,0:T(8,128)(2,1)S(1)} %add_convert_fusion.2), channel_id=1, source_target_pairs={{1,0},{2,1},{3,2},{0,3},{5,4},{6,5},{7,6},{4,7},{9,8},{10,9},{11,1... | collective-permute-start | bytes 393224 | tf_op jit(solution)/shard_map/ppermute | solution.py:344
  44.2 6.8 %collective-permute-start.9 = (bf16[4,128,128]{2,1,0:T(8,128)(2,1)S(1)}, bf16[4,128,128]{2,1,0:T(8,128)(2,1)S(1)}, u32[]{:S(2)}, u32[]{:S(2)}) collective-permute-start(bf16[4,128,128]{2,1,0:T(8,128)(2,1)S(1)} %add_convert_fusion.3), channel_id=1, source_target_pairs={{0,1},{1,2},{2,3},{3,0},{4,5},{5,6},{6,7},{7,4},{8,9},{9,10},{10,1... | collective-permute-start | bytes 393224 | tf_op jit(solution)/shard_map/ppermute | solution.py:344
  51.1 10.2 %copy-start.3 = (bf16[128,128]{1,0:T(8,128)(2,1)S(1)}, bf16[128,128]{1,0:T(8,128)(2,1)}, u32[]{:S(2)}) copy-start(bf16[128,128]{1,0:T(8,128)(2,1)} %refs_2_.1) | copy-start | bytes 98308
  52.1 9.2 %collective-permute-start.11 = (bf16[8,128,128]{2,1,0:T(8,128)(2,1)S(1)}, bf16[8,128,128]{2,1,0:T(8,128)(2,1)S(1)}, u32[]{:S(2)}, u32[]{:S(2)}) collective-permute-start(bf16[8,128,128]{2,1,0:T(8,128)(2,1)S(1)} %get-tuple-element.44.refs_0_), channel_id=1, source_target_pairs={{0,4},{1,5},{2,6},{3,7},{4,0},{5,1},{6,2},{7,3},{8,12},{9,13},{10,... | collective-permute-start | bytes 786440 | tf_op jit(solution)/shard_map/ppermute | solution.py:349
  62.5 7.4 %collective-permute-start.12 = (bf16[9,128,128]{2,1,0:T(8,128)(2,1)S(1)}, bf16[9,128,128]{2,1,0:T(8,128)(2,1)S(1)}, u32[]{:S(2)}, u32[]{:S(2)}) collective-permute-start(bf16[9,128,128]{2,1,0:T(8,128)(2,1)S(1)} %get-tuple-element.48.refs_5_.refs_8_), channel_id=1, source_target_pairs={{1,0},{2,1},{3,2},{0,3},{5,4},{6,5},{7,6},{4,7},{9,8},{10,9},{11,1... | collective-permute-start | bytes 884744 | tf_op jit(solution)/shard_map/ppermute | solution.py:344
  62.8 9.2 %collective-permute-start.13 = (bf16[9,128,128]{2,1,0:T(8,128)(2,1)S(1)}, bf16[9,128,128]{2,1,0:T(8,128)(2,1)S(1)}, u32[]{:S(2)}, u32[]{:S(2)}) collective-permute-start(bf16[9,128,128]{2,1,0:T(8,128)(2,1)S(1)} %get-tuple-element.48.refs_5_.refs_8_), channel_id=1, source_target_pairs={{0,1},{1,2},{2,3},{3,0},{4,5},{5,6},{6,7},{7,4},{8,9},{9,10},{10,1... | collective-permute-start | bytes 884744 | tf_op jit(solution)/shard_map/ppermute | solution.py:344
  70.0 8.2 %collective-permute-start.15 = (bf16[5,128,128]{2,1,0:T(8,128)(2,1)S(1)}, bf16[5,128,128]{2,1,0:T(8,128)(2,1)S(1)}, u32[]{:S(2)}, u32[]{:S(2)}) collective-permute-start(bf16[5,128,128]{2,1,0:T(8,128)(2,1)S(1)} %slice.27), channel_id=1, source_target_pairs={{1,0},{2,1},{3,2},{0,3},{5,4},{6,5},{7,6},{4,7},{9,8},{10,9},{11,1... | collective-permute-start | bytes 491528 | tf_op jit(solution)/shard_map/ppermute | solution.py:344
  71.9 6.2 %collective-permute-start.14 = (bf16[4,128,128]{2,1,0:T(8,128)(2,1)S(1)}, bf16[4,128,128]{2,1,0:T(8,128)(2,1)S(1)}, u32[]{:S(2)}, u32[]{:S(2)}) collective-permute-start(bf16[4,128,128]{2,1,0:T(8,128)(2,1)S(1)} %slice.26), channel_id=1, source_target_pairs={{0,1},{1,2},{2,3},{3,0},{4,5},{5,6},{6,7},{7,4},{8,9},{9,10},{10,1... | collective-permute-start | bytes 393224 | tf_op jit(solution)/shard_map/ppermute | solution.py:344
  79.9 2.8 %collective-permute-start.16 = (bf16[33,128,128]{2,1,0:T(8,128)(2,1)S(1)}, bf16[33,128,128]{2,1,0:T(8,128)(2,1)S(1)}, u32[]{:S(2)}, u32[]{:S(2)}) collective-permute-start(bf16[33,128,128]{2,1,0:T(8,128)(2,1)S(1)} %get-tuple-element.49), channel_id=1, source_target_pairs={{0,8},{8,0},{16,24},{24,16},{32,40},{40,32},{48,56},{56,48},{64,72... | collective-permute-start | bytes 3244040 | tf_op jit(solution)/shard_map/ppermute | solution.py:349
  82.8 13.1 %collective-permute-start.18 = (bf16[9,128,128]{2,1,0:T(8,128)(2,1)S(1)}, bf16[9,128,128]{2,1,0:T(8,128)(2,1)S(1)}, u32[]{:S(2)}, u32[]{:S(2)}) collective-permute-start(bf16[9,128,128]{2,1,0:T(8,128)(2,1)S(1)} %get-tuple-element.53), channel_id=1, source_target_pairs={{32,0},{40,8},{48,16},{56,24},{64,32},{72,40},{80,48},{88,56},{96,... | collective-permute-start | bytes 884744 | tf_op jit(solution)/shard_map/ppermute | solution.py:344
  87.0 8.8 %collective-permute-start.17 = (bf16[9,128,128]{2,1,0:T(8,128)(2,1)S(1)}, bf16[9,128,128]{2,1,0:T(8,128)(2,1)S(1)}, u32[]{:S(2)}, u32[]{:S(2)}) collective-permute-start(bf16[9,128,128]{2,1,0:T(8,128)(2,1)S(1)} %get-tuple-element.52.refs_5_), channel_id=1, source_target_pairs={{0,32},{8,40},{16,48},{24,56},{32,64},{40,72},{48,80},{56,88},{64,... | collective-permute-start | bytes 884744 | tf_op jit(solution)/shard_map/ppermute | solution.py:344
  95.9 6.6 %collective-permute-start.19 = (bf16[5,128,128]{2,1,0:T(8,128)(2,1)S(1)}, bf16[5,128,128]{2,1,0:T(8,128)(2,1)S(1)}, u32[]{:S(2)}, u32[]{:S(2)}) collective-permute-start(bf16[5,128,128]{2,1,0:T(8,128)(2,1)S(1)} %add_convert_fusion), channel_id=1, source_target_pairs={{0,32},{8,40},{16,48},{24,56},{32,64},{40,72},{48,80},{56,88},{64,... | collective-permute-start | bytes 491528 | tf_op jit(solution)/shard_map/ppermute | solution.py:344
  96.0 5.8 %collective-permute-start.20 = (bf16[4,128,128]{2,1,0:T(8,128)(2,1)S(1)}, bf16[4,128,128]{2,1,0:T(8,128)(2,1)S(1)}, u32[]{:S(2)}, u32[]{:S(2)}) collective-permute-start(bf16[4,128,128]{2,1,0:T(8,128)(2,1)S(1)} %add_convert_fusion.1), channel_id=1, source_target_pairs={{32,0},{40,8},{48,16},{56,24},{64,32},{72,40},{80,48},{88,56},{96,... | collective-permute-start | bytes 393224 | tf_op jit(solution)/shard_map/ppermute | solution.py:344
  102.5 5.4 %collective-permute-start.21 = (bf16[5,128,128]{2,1,0:T(8,128)(2,1)S(1)}, bf16[5,128,128]{2,1,0:T(8,128)(2,1)S(1)}, u32[]{:S(2)}, u32[]{:S(2)}) collective-permute-start(bf16[5,128,128]{2,1,0:T(8,128)(2,1)S(1)} %far_columns.1.refs_5_), channel_id=1, source_target_pairs={{0,16},{8,24},{16,0},{24,8},{32,48},{40,56},{48,32},{56,40},{64,80... | collective-permute-start | bytes 491528 | tf_op jit(solution)/shard_map/ppermute | solution.py:349
